TPU v7x, 128 devices: a whole 4x4x4 slice. The times are simulated.
128 devices in a mesh: row: 16 (over x, z_lo, core), col: 8 (over y, z_hi).
Axes of the slice: x: 4, y: 4, z: 4 (z_hi: 2, z_lo: 2; z = z_hi * 2 + z_lo), core: 2. Of those that a mesh axis runs over, the one named last changes fastest.
Arguments:
- built: bfloat16 [8192, 8192], P('row', 'col'), may hold values from -0.59765625 to 0.59765625
- build_order: int32 [64], replicated, may hold values from 0 to 63, each once
- p_pattern: int32 [64, 64], replicated, may hold values from 0 to 1, as said below
- q_pattern: int32 [64, 64], replicated, may hold values from 0 to 1, as said below
Outputs:
- purified: bfloat16 [8192, 8192], P('row', 'col')
Inputs may be any that keep to these rules, and one draw needn't show every extreme that they name: p_pattern is symmetric and 1 on the diagonal; p_pattern[i, j] is 0 unless the distance of i and j counted round the 64 blocks, or that of i and j + 32, is at most 1. q_pattern[i, j] is 0 unless the distance of i and j counted round the 64 blocks, or that of i and j + 32, is at most 2.
All inputs are finite; a program needn't handle non-finite values.
Results may differ from a plain program's by a relative error of at most 0.0045.
Values may be sent and summed in bfloat16 or wider, within the bound.
No kernel may reach another device: no remote copies, remote signals or barrier semaphores. Data moves between devices by JAX's collectives and lax.ppermute only.
A program may use at most 128 MiB of HBM per device.

v0:
```python
import jax
import jax.numpy as jnp
from jax import lax
from jax.sharding import PartitionSpec as P

BS = 128


def contract(col_panel, portion):
    return jnp.dot(portion, col_panel, preferred_element_type=jnp.float32)


def body(built, build_order, p_pattern, q_pattern):
    row_count = built.shape[0] // BS
    col_count = built.shape[1] // BS
    block_count = build_order.shape[0]
    row_index = lax.axis_index("row")
    col_index = lax.axis_index("col")
    build_slab = lax.all_gather(built, "row", axis=0, tiled=True)
    blocks = build_slab.reshape(block_count, BS, col_count * BS)
    inverse = (
        jnp.zeros((block_count,), jnp.int32)
        .at[build_order]
        .set(jnp.arange(block_count, dtype=jnp.int32))
    )
    col_mask = lax.dynamic_slice_in_dim(p_pattern, col_index * col_count, col_count, 1).astype(
        jnp.bfloat16
    )
    ordered = blocks[inverse].reshape(block_count, BS, col_count, BS)
    columns = (ordered * col_mask[:, None, :, None]).reshape(block_count * BS, col_count * BS)
    start_block = row_index * row_count
    local_tile = lax.dynamic_slice_in_dim(columns, start_block * BS, row_count * BS, 0)
    q_block = lax.dynamic_slice(
        q_pattern, (start_block, col_index * col_count), (row_count, col_count)
    ).astype(jnp.float32)
    q_tile = jnp.broadcast_to(q_block[:, None, :, None], (row_count, BS, col_count, BS)).reshape(
        row_count * BS, col_count * BS
    )
    square = contract(columns, lax.all_gather(local_tile, "col", axis=1, tiled=True)) * q_tile
    rounded = square.astype(jnp.bfloat16)
    cubed_term = contract(columns, lax.all_gather(rounded, "col", axis=1, tiled=True))
    return ((3.0 * square - 2.0 * cubed_term) * q_tile).astype(jnp.bfloat16)


def solution(mesh):
    placed = (P("row", "col"), P(), P(), P())
    return jax.shard_map(
        body, mesh=mesh, in_specs=placed, out_specs=P("row", "col"), check_vma=False
    )
```

profile of v0, /device:TPU:1, one launch (start us, length us, event | category | flops | bytes accessed | tf_op | source)
XLA Modules:
  0.0 387.4 jit_solution(14964516549320403365)
XLA Ops:
  6.5 0.0 all-gather.4.cloned.1.call-start
  6.5 0.7 all-gather.4.cloned.1.call-update
  7.3 0.0 all-gather.6.cloned.1.call-start
  7.3 0.7 compare_select_fusion.1
  8.0 0.8 scatter_custom_fusion
  8.8 0.8 dynamic-slice_convert_fusion
  9.6 94.8 %all-gather.4.cloned.1.call-done = bf16[8192,1024]{1,0:T(8,128)(2,1)} async-done(((bf16[512,1024]{1,0:T(8,128)(2,1)}), bf16[8192,1024]{1,0:T(8,128)(2,1)}) %all-gather.4.cloned.1.call-update) | async-done | bytes 16777232 | tf_op jit(solution)/shard_map/all_gather | solution.py:19
  104.4 13.4 %gather_fusion = bf16[64,128,1024]{2,1,0:T(8,128)(2,1)} fusion(bf16[64,128,1024]{2,1,0:T(8,128)(2,1)} %bitcast.23, s32[1024]{0:T(1024)S(1)} %pad_clamp_fusion), kind=kCustom, calls=%fused_computation | custom fusion | bytes 33554688 | tf_op jit(solution)/shard_map/gather | solution.py:29
  117.8 0.0 copy-start
  117.8 2.8 mul.40
  120.6 3.0 copy-done
  123.6 6.5 %bitcast_multiply_fusion = bf16[8192,1024]{1,0:T(8,128)(2,1)} fusion(bf16[1024,8,8,128]{3,2,1,0:T(8,128)(2,1)S(1)} %bitcast.22, bf16[64,128,1024]{2,1,0:T(8,128)(2,1)S(1)} %copy-done), kind=kLoop, calls=%fused_computation.2 | loop fusion | flops 8388608 | bytes 50331648 | tf_op jit(solution)/shard_map/mul | solution.py:30
  130.1 2.3 constant_dynamic-slice_fusion
  132.3 0.0 all-gather.6.cloned.1.call-update
  132.4 0.0 all-gather.8.cloned.1.call-start
  132.4 0.8 dynamic-slice_convert_fusion.1
  133.2 108.2 %all-gather.6.cloned.1.call-done = bf16[512,8192]{1,0:T(8,128)(2,1)} async-done(((bf16[512,1024]{1,0:T(8,128)(2,1)}), bf16[512,8192]{1,0:T(8,128)(2,1)}) %all-gather.6.cloned.1.call-update) | async-done | bytes 8388624 | tf_op jit(solution)/shard_map/all_gather | solution.py:39
  241.4 0.2 broadcast_in_dim.15
  241.6 16.2 %fusion.1 = (bf16[512,1024]{1,0:T(8,128)(2,1)}, f32[512,1024]{1,0:T(8,128)}) fusion(f32[64,8,8,128]{3,2,1,0:T(8,128)S(1)} %bitcast.24, bf16[512,8192]{1,0:T(8,128)(2,1)} %all-gather.6.cloned.1.call-done, bf16[8192,1024]{1,0:T(8,128)(2,1)} %bitcast_multiply_fusion), kind=kOutput, calls=%fused_computation.6 | convolution fusion | flops 8590983168 | bytes 30408704 | tf_op jit(solution)/shard_map/dot_general | solution.py:10
  257.7 0.0 all-gather.8.cloned.1.call-update
  257.8 106.8 %all-gather.8.cloned.1.call-done = bf16[512,8192]{1,0:T(8,128)(2,1)} async-done(((bf16[512,1024]{1,0:T(8,128)(2,1)}), bf16[512,8192]{1,0:T(8,128)(2,1)}) %all-gather.8.cloned.1.call-update) | async-done | bytes 8388624 | tf_op jit(solution)/shard_map/all_gather | solution.py:41
  364.6 16.3 %fusion = bf16[512,1024]{1,0:T(8,128)(2,1)} fusion(f32[64,8,8,128]{3,2,1,0:T(8,128)S(1)} %bitcast.25, f32[512,1024]{1,0:T(8,128)} %get-tuple-element.6, bf16[512,8192]{1,0:T(8,128)(2,1)} %all-gather.8.cloned.1.call-done, bf16[8192,1024]{1,0:T(8,128)(2,1)} %bitcast_multiply_fusion), kind=kOutput, calls=%fused_computation.5 | convolution fusion | flops 8593080320 | bytes 30408704 | tf_op jit(solution)/shard_map/dot_general | solution.py:10
  (3 shorter events, 0.0 us)
Async XLA Ops:
  6.5 97.9 %all-gather.4.cloned.1.call-start = ((), (), s32[]{:S(2)}) async-start(), calls=%async_computation | async-start | bytes 17825792 | tf_op jit(solution)/shard_map/all_gather | solution.py:19
  7.3 234.1 %all-gather.6.cloned.1.call-start = ((), (), s32[]{:S(2)}) async-start(), calls=%async_computation.1 | async-start | bytes 9437184 | tf_op jit(solution)/shard_map/all_gather | solution.py:39
  117.8 5.8 %copy-start = (bf16[64,128,1024]{2,1,0:T(8,128)(2,1)S(1)}, bf16[64,128,1024]{2,1,0:T(8,128)(2,1)}, u32[]{:S(2)}) copy-start(bf16[64,128,1024]{2,1,0:T(8,128)(2,1)} %gather_fusion) | copy-start | bytes 50331652
  132.4 232.2 %all-gather.8.cloned.1.call-start = ((), (), s32[]{:S(2)}) async-start(), calls=%async_computation.2 | async-start | bytes 9437184 | tf_op jit(solution)/shard_map/all_gather | solution.py:41
Sparse Core Ops, SparseCore 0:
  9.1 95.2 all-gather.3
  132.5 108.8 all-gather.5
  257.9 106.6 all-gather.7
where the time goes:
time: 388 us; the launch traced here: 387 us
  waiting for transfers between devices  310 us (80%)
  matrix products  32.4 us (8%)
  local copies, waits for them, and re-layouts  22.4 us (6%)
  between operations  13.2 us (3%)
  other arithmetic  8.79 us (2%)
    all_gather x1, waiting for transfers between devices, body(): lax.all_gather(local_tile, 'col', axis=1, tiled=True)  108 us
    all_gather x1, waiting for transfers between devices, body(): lax.all_gather(rounded, 'col', axis=1, tiled=True)  107 us
    all_gather x1, waiting for transfers between devices, body(): build_slab = lax.all_gather(built, 'row', axis=0, tiled=True)  94.8 us
    dot_general x2, matrix products, contract(): return jnp.dot(portion, col_panel, preferred_element_type=jnp.float32)  32.4 us
    gather x1, local copies, waits for them, and re-layouts, body(): ordered = blocks[inverse].reshape(block_count, BS, col_count, BS)  13.4 us
  transfers between devices with their start and end apart: 3, of which 3 were waited for; matrix products, arithmetic and copies ran while one was open for 1% of the time, Pallas kernels for 0%

commit v1 on v0

v1 whole, which is shorter than its diff:
```python
import functools

import jax
import jax.numpy as jnp
import numpy as np
from jax import lax
from jax.experimental import pallas as pl
from jax.experimental.pallas import tpu as pltpu
from jax.sharding import Mesh
from jax.sharding import PartitionSpec as P

BS = 128
GRID = (4, 2, 2, 2, 2, 2)
AXES = ("x", "zl", "core", "yh", "yl", "zh")
ROW = ("x", "zl", "core")
COL = ("yh", "yl", "zh")
CHIPS = 8
PART = BS // CHIPS
WIN = 13
PLACES = [(b + e, b) for b in range(-2, 3) for e in (-1, 0, 1) if abs(b + e) <= 2]
SLOT = {rc: n for n, rc in enumerate(PLACES)}

VMEM = pl.BlockSpec(memory_space=pltpu.VMEM)
SMEM = pl.BlockSpec(memory_space=pltpu.SMEM)
HBM = pl.BlockSpec(memory_space=pl.ANY)
PARAMS = pltpu.CompilerParams(vmem_limit_bytes=48 * 1024 * 1024)


def chip_index():
    return lax.axis_index("x") * 2 + lax.axis_index("zl")


def group_index():
    return lax.axis_index("yl") * 2 + lax.axis_index("zh")


def pick_kernel(order, built, out, sem):
    first = (chip_index() * 2 + lax.axis_index("core")) * 4
    copies = []
    for k in range(4):
        row = order[first + k]
        for d in range(3):
            col = lax.rem(row + d + 31, 8)
            at = pl.ds(pl.multiple_of(col * BS, BS), BS)
            copies.append(
                pltpu.make_async_copy(
                    built.at[k, :, :, at], out.at[:, 3 * k + d], sem.at[3 * k + d]
                )
            )
            copies[-1].start()
    for copy in copies:
        copy.wait()


def place_kernel(order, pattern, mine, other, out, inverse):
    for k in range(64):
        inverse[order[k]] = k
    core = lax.axis_index("core")
    yh = lax.axis_index("yh")
    base = group_index() * 8
    for bl in range(8):
        for e in range(3):
            row = lax.rem(base + bl + e + 31, 32) + 32 * core
            at = inverse[row]
            device = at // 4
            slot = lax.rem(at, 4) * 3 + (2 - e)
            chip = device // 2
            here = lax.rem(device, 2) == core
            keep = pattern[row, base + bl + 32 * yh] != 0
            value = jnp.where(here, mine[chip, slot], other[chip, slot])
            out[3 * bl + e] = jnp.where(keep, value, jnp.zeros_like(value))


def window_kernel(left, own, right, out):
    def piece(first, last):
        for ref, lo, hi in ((left, 0, 5), (own, 5, 29), (right, 29, 34)):
            a, b = max(first, lo), min(last, hi)
            if a < b:
                yield a, b, ref[a - lo : b - lo]

    for q in range(CHIPS):
        for a, b, value in piece(3 * q, 3 * q + WIN):
            for half in range(2):
                out[2 * q + half, a - 3 * q : b - 3 * q] = value


def purify_kernel(pattern, mine, other, rows_out, near_out, far_out, blocks):
    core = lax.axis_index("core")
    yh = lax.axis_index("yh")
    q = chip_index()
    middle = group_index() * 8 + q
    for n in range(WIN):
        for chip in range(CHIPS):
            for half in range(2):
                at = pl.ds(chip * PART, PART)
                blocks[n, half, core, at] = mine[2 * chip + half, n]
                blocks[n, half, 1 - core, at] = other[2 * chip + half, n]

    def whole(row, col):
        n = SLOT[row, col]
        return jnp.concatenate(
            [blocks[n, 0].reshape(2 * BS, BS), blocks[n, 1].reshape(2 * BS, BS)], 1
        )

    def left(col):
        n = SLOT[0, col]
        return jnp.concatenate([blocks[n, 0, core], blocks[n, 1, core]], 1)

    def dot(a, b):
        return jnp.dot(a, b, preferred_element_type=jnp.float32)

    row = middle + 32 * core
    squares, rounded = [], []
    for k in range(-2, 3):
        total = None
        for l in range(-1, 2):
            if abs(l - k) <= 1:
                term = dot(left(l), whole(l, k))
                total = term if total is None else total + term
        col = lax.rem(middle + k + 32, 32)
        halves = []
        for half in range(2):
            part = total[:, half * BS : (half + 1) * BS]
            keep = pattern[row, col + 32 * half] != 0
            halves.append(jnp.where(keep, part, jnp.zeros_like(part)))
        squares.append(jnp.where(yh == 0, halves[0], halves[1]))
        rounded.append(jnp.concatenate(halves, 1).astype(jnp.bfloat16))
    results = []
    for j in range(-2, 3):
        total = None
        for k in range(-2, 3):
            if abs(k - j) <= 1:
                term = dot(rounded[k + 2], blocks[SLOT[k, j], yh].reshape(2 * BS, BS))
                total = term if total is None else total + term
        col = lax.rem(middle + j + 32, 32)
        keep = pattern[row, col + 32 * yh] != 0
        value = 3.0 * squares[j + 2] - 2.0 * total
        results.append(jnp.where(keep, value, jnp.zeros_like(value)).astype(jnp.bfloat16))
        rows_out[j + 2] = results[-1]
    low = q < 4
    near_out[0] = jnp.where(low, results[0], results[3])
    near_out[1] = jnp.where(low, results[1], results[4])
    far_out[0] = jnp.where(low, results[0], results[4])


def output_kernel(r0, r1, r2, r3, near, far, out):
    out[...] = jnp.zeros_like(out)
    core = lax.axis_index("core")
    away = lax.rem(chip_index() - group_index() + 8, 4)

    def put(row, col, value):
        out[row * BS : (row + 1) * BS, col * BS : (col + 1) * BS] = value

    for u in range(2):

        @pl.when(jnp.logical_and(away == 0, core == u))
        def _(u=u):
            for s, ref in enumerate((r0, r1, r2, r3)):
                for n in range(5):
                    col = 4 * u + s + n - 2
                    if 0 <= col < 8:
                        put(s, col, ref[n])

    @pl.when(jnp.logical_and(away == 1, core == 0))
    def _():
        put(0, 6, near[0])
        put(0, 7, near[1])
        put(1, 7, far[0])

    @pl.when(jnp.logical_and(away == 3, core == 1))
    def _():
        put(2, 0, far[0])
        put(3, 0, near[0])
        put(3, 1, near[1])


def device(q, core, yh, g):
    return ((q * 2 + core) * 2 + yh) * 4 + g % 4


PLANES = [(core, yh, g) for core in range(2) for yh in range(2) for g in range(4)]


def to_rows(s):
    return [
        (device(4 * u + s, core, yh, g), device(g + 4 * core, u, yh, g))
        for core, yh, g in PLANES
        for u in range(2)
    ]


def to_corners(low, high):
    return [
        (device(q, core, yh, g), device(g + 4 * core, u, yh, g + step))
        for core, yh, g in PLANES
        for q, u, step in ((low, 0, -1), (high, 1, 1))
    ]


def call(kernel, shape, specs, out_spec=VMEM, scratch=()):
    make = lambda s: jax.ShapeDtypeStruct(s, jnp.bfloat16)
    many = isinstance(shape, list)
    return pl.pallas_call(
        kernel,
        out_shape=[make(s) for s in shape] if many else make(shape),
        in_specs=specs,
        out_specs=[out_spec] * len(shape) if many else out_spec,
        scratch_shapes=list(scratch),
        compiler_params=PARAMS,
    )


def swap_cores(a):
    return lax.ppermute(a, "core", [(0, 1), (1, 0)])


def body(built, build_order, p_pattern, q_pattern):
    parts = call(
        pick_kernel,
        (CHIPS, 12, PART, BS),
        [SMEM, HBM],
        HBM,
        [pltpu.SemaphoreType.DMA((12,))],
    )(build_order, built.reshape(4, CHIPS, PART, 8 * BS))
    parts = lax.all_to_all(parts, ("x", "zl"), 0, 0, tiled=True)
    placed = call(
        place_kernel,
        (24, PART, BS),
        [SMEM, SMEM, VMEM, VMEM],
        scratch=[pltpu.SMEM((64,), jnp.int32)],
    )(build_order, p_pattern, parts, swap_cores(parts))
    right_of = [(g, (g + 1) % 4) for g in range(4)]
    left = lax.ppermute(placed[19:], ("yl", "zh"), right_of)
    right = lax.ppermute(placed[:5], ("yl", "zh"), [(b, a) for a, b in right_of])
    windows = call(window_kernel, (2 * CHIPS, WIN, PART, BS), [VMEM] * 3)(left, placed, right)
    windows = lax.all_to_all(windows, ("x", "zl", "yh"), 0, 0, tiled=True)
    rows, near, far = call(
        purify_kernel,
        [(5, BS, BS), (2, BS, BS), (1, BS, BS)],
        [SMEM, VMEM, VMEM],
        scratch=[pltpu.VMEM((WIN, 2, 2, BS, BS), jnp.bfloat16)],
    )(q_pattern, windows, swap_cores(windows))
    near = lax.ppermute(near, AXES, to_corners(0, 7))
    far = lax.ppermute(far, AXES, to_corners(1, 6))
    sent = [lax.ppermute(rows, AXES, to_rows(s)) for s in range(4)]
    return call(output_kernel, (4 * BS, 8 * BS), [VMEM] * 6)(*sent, near, far)


def solution(mesh):
    fine = Mesh(mesh.devices.reshape(GRID), AXES)
    placed = (P(ROW, COL), P(), P(), P())
    return jax.shard_map(
        body, mesh=fine, in_specs=placed, out_specs=P(ROW, COL), check_vma=False
    )
```

time: 388 us -> 81.7 us (0.21)
  the two profiles are of different devices: /device:TPU:1 before, /device:TPU:41 now
where the time goes in v1:
time: 81.7 us; the launch traced here: 81.2 us
  blocking collectives  30.7 us (38%)
  waiting for transfers between devices  23.1 us (28%)
  starting transfers between devices  20 us (24%)
  Pallas kernels  5.45 us (7%)
  local copies, waits for them, and re-layouts  1.9 us (2%)
    all_to_all x1, blocking collectives, body(): windows = lax.all_to_all(windows, ('x', 'zl', 'yh'), 0, 0, tiled=True)  18.8 us
    all_to_all x1, blocking collectives, body(): parts = lax.all_to_all(parts, ('x', 'zl'), 0, 0, tiled=True)  11.9 us
    ppermute x4, starting transfers between devices, body(): sent = [lax.ppermute(rows, AXES, to_rows(s)) for s in range(4)]  8.99 us
    ppermute x1, waiting for transfers between devices, body(): near = lax.ppermute(near, AXES, to_corners(0, 7))  8.8 us
    ppermute x1, waiting for transfers between devices, body(): far = lax.ppermute(far, AXES, to_corners(1, 6))  6.31 us
    ppermute x2, starting transfers between devices, swap_cores(): return lax.ppermute(a, 'core', [(0, 1), (1, 0)])  4.73 us
    ppermute x1, waiting for transfers between devices, body(): left = lax.ppermute(placed[19:], ('yl', 'zh'), right_of)  3.48 us
    ppermute x2, waiting for transfers between devices, swap_cores(): return lax.ppermute(a, 'core', [(0, 1), (1, 0)])  3.36 us
  transfers between devices with their start and end apart: 10, of which 6 were waited for; matrix products, arithmetic and copies ran while one was open for 0% of the time, Pallas kernels for 0%

profile of v1, /device:TPU:41, one launch (start us, length us, event | category | flops | bytes accessed | tf_op | source)
XLA Modules:
  0.0 81.2 jit_solution(12597221952089865245)
XLA Ops:
  0.0 0.0 copy-start.3
  0.0 0.7 copy-done.3
  0.7 0.0 copy-start
  0.7 1.2 %copy-done = bf16[512,1024]{1,0:T(8,128)(2,1)S(1)} copy-done((bf16[512,1024]{1,0:T(8,128)(2,1)S(1)}, bf16[512,1024]{1,0:T(8,128)(2,1)}, u32[]{:S(2)}) %copy-start) | copy-done | bytes 1048600
  1.9 0.9 %shard_map.46 = bf16[8,12,16,128]{3,2,1,0:T(8,128)(2,1)S(1)} custom-call(s32[64]{0:T(128)S(1)} %copy-done.3, bf16[4,8,16,1024]{3,2,1,0:T(8,128)(2,1)S(1)} %bitcast.1), custom_call_target="tpu_custom_call" | custom-call | tf_op jit(solution)/shard_map/pallas_call | solution.py:218
  2.8 0.0 copy-start.1
  2.8 11.9 %all_to_all.10.mine = bf16[8,12,16,128]{3,2,1,0:T(8,128)(2,1)S(1)} all-to-all(bf16[8,12,16,128]{3,2,1,0:T(8,128)(2,1)S(1)} %shard_map.46), channel_id=1, replica_groups=mesh['x'=4,'zl'=2,'core'=2,'yh'=2,'yl'=2,'zh'=2] {'x','zl'}, dimensions={0} | all-to-all | bytes 786432 | tf_op jit(solution)/shard_map/all_to_all | solution.py:225
  14.6 1.9 %collective-permute-start = (bf16[8,12,16,128]{3,2,1,0:T(8,128)(2,1)S(1)}, bf16[8,12,16,128]{3,2,1,0:T(8,128)(2,1)S(1)}, u32[]{:S(2)}, u32[]{:S(2)}) collective-permute-start(bf16[8,12,16,128]{3,2,1,0:T(8,128)(2,1)S(1)} %all_to_all.10.mine), channel_id=1, source_target_pairs={{0,8},{8,0},{1,9},{9,1},{2,10},{10,2},{3,11},{11,3},{4,12},{12,4},... | collective-permute-start | bytes 1179656 | tf_op jit(solution)/shard_map/ppermute | solution.py:214
  16.5 1.3 %collective-permute-done.other = bf16[8,12,16,128]{3,2,1,0:T(8,128)(2,1)S(1)} collective-permute-done((bf16[8,12,16,128]{3,2,1,0:T(8,128)(2,1)S(1)}, bf16[8,12,16,128]{3,2,1,0:T(8,128)(2,1)S(1)}, u32[]{:S(2)}, u32[]{:S(2)}) %collective-permute-start) | collective-permute-done | bytes 393248 | tf_op jit(solution)/shard_map/ppermute | solution.py:214
  17.9 0.0 copy-done.1
  17.9 1.5 %shard_map.47.own = bf16[24,16,128]{2,1,0:T(8,128)(2,1)S(1)} custom-call(s32[64]{0:T(128)S(1)} %copy-done.3, s32[64,64]{1,0:T(8,128)S(1)} %copy-done.1, bf16[8,12,16,128]{3,2,1,0:T(8,128)(2,1)S(1)} %all_to_all.10.mine, bf16[8,12,16,128]{3,2,1,0:T(8,128)(2,1)S(1)} %collective-permute-done.other), custom_call_target="tpu_custom_call" | custom-call | tf_op jit(solution)/shard_map/pallas_call | solution.py:226
  19.4 2.7 %collective-permute-start.2 = (bf16[5,16,128]{2,1,0:T(8,128)(2,1)S(1)}, bf16[5,16,128]{2,1,0:T(8,128)(2,1)S(1)}, u32[]{:S(2)}, u32[]{:S(2)}) collective-permute-start(bf16[5,16,128]{2,1,0:T(8,128)(2,1)S(1)} %get-tuple-element.11), channel_id=1, source_target_pairs={{1,0},{2,1},{3,2},{0,3},{5,4},{6,5},{7,6},{4,7},{9,8},{10,9},{11,1... | collective-permute-start | bytes 61448 | tf_op jit(solution)/shard_map/ppermute | solution.py:234
  22.0 0.4 collective-permute-start.1
  22.4 1.2 %collective-permute-done.2.right = bf16[5,16,128]{2,1,0:T(8,128)(2,1)S(1)} collective-permute-done((bf16[5,16,128]{2,1,0:T(8,128)(2,1)S(1)}, bf16[5,16,128]{2,1,0:T(8,128)(2,1)S(1)}, u32[]{:S(2)}, u32[]{:S(2)}) %collective-permute-start.2) | collective-permute-done | bytes 20512 | tf_op jit(solution)/shard_map/ppermute | solution.py:234
  23.6 3.5 %collective-permute-done.1.left = bf16[5,16,128]{2,1,0:T(8,128)(2,1)S(1)} collective-permute-done((bf16[5,16,128]{2,1,0:T(8,128)(2,1)S(1)}, bf16[5,16,128]{2,1,0:T(8,128)(2,1)S(1)}, u32[]{:S(2)}, u32[]{:S(2)}) %collective-permute-start.1) | collective-permute-done | bytes 20512 | tf_op jit(solution)/shard_map/ppermute | solution.py:233
  27.1 0.1 shard_map.48
  27.2 0.0 copy-start.2
  27.2 18.8 %all_to_all.11.mine = bf16[16,13,16,128]{3,2,1,0:T(8,128)(2,1)S(1)} all-to-all(bf16[16,13,16,128]{3,2,1,0:T(8,128)(2,1)S(1)} %shard_map.48), channel_id=1, replica_groups=mesh['x'=4,'zl'=2,'core'=2,'yh'=2,'yl'=2,'zh'=2] {'x','zl','yh'}, dimensions={0} | all-to-all | bytes 1703936 | tf_op jit(solution)/shard_map/all_to_all | solution.py:236
  46.0 2.9 %collective-permute-start.3 = (bf16[16,13,16,128]{3,2,1,0:T(8,128)(2,1)S(1)}, bf16[16,13,16,128]{3,2,1,0:T(8,128)(2,1)S(1)}, u32[]{:S(2)}, u32[]{:S(2)}) collective-permute-start(bf16[16,13,16,128]{3,2,1,0:T(8,128)(2,1)S(1)} %all_to_all.11.mine), channel_id=1, source_target_pairs={{0,8},{8,0},{1,9},{9,1},{2,10},{10,2},{3,11},{11,3},{4,12},{12,4},... | collective-permute-start | bytes 2555912 | tf_op jit(solution)/shard_map/ppermute | solution.py:214
  48.9 2.0 %collective-permute-done.3.other = bf16[16,13,16,128]{3,2,1,0:T(8,128)(2,1)S(1)} collective-permute-done((bf16[16,13,16,128]{3,2,1,0:T(8,128)(2,1)S(1)}, bf16[16,13,16,128]{3,2,1,0:T(8,128)(2,1)S(1)}, u32[]{:S(2)}, u32[]{:S(2)}) %collective-permute-start.3) | collective-permute-done | bytes 852000 | tf_op jit(solution)/shard_map/ppermute | solution.py:214
  50.9 0.0 copy-done.2
  50.9 1.9 %shard_map.49 = (bf16[5,128,128]{2,1,0:T(8,128)(2,1)S(1)}, bf16[2,128,128]{2,1,0:T(8,128)(2,1)S(1)}, bf16[1,128,128]{2,1,0:T(8,128)(2,1)S(1)}) custom-call(s32[64,64]{1,0:T(8,128)S(1)} %copy-done.2, bf16[16,13,16,128]{3,2,1,0:T(8,128)(2,1)S(1)} %all_to_all.11.mine, bf16[16,13,16,128]{3,2,1,0:T(8,128)(2,1)S(1)} %collective-permute-done.3.other), custom_call_target="tpu_custom_call" | custom-call | tf_op jit(solution)/shard_map/pallas_call | solution.py:237
  52.8 0.7 collective-permute-start.7
  53.5 0.7 collective-permute-start.6
  54.1 7.0 %collective-permute-start.5 = (bf16[5,128,128]{2,1,0:T(8,128)(2,1)S(1)}, bf16[5,128,128]{2,1,0:T(8,128)(2,1)S(1)}, u32[]{:S(2)}, u32[]{:S(2)}) collective-permute-start(bf16[5,128,128]{2,1,0:T(8,128)(2,1)S(1)} %get-tuple-element.8), channel_id=1, source_target_pairs={{16,0},{80,8},{17,17},{81,25},{18,34},{82,42},{19,51},{83,59},{20,... | collective-permute-start | bytes 491528 | tf_op jit(solution)/shard_map/ppermute | solution.py:245
  61.1 0.7 collective-permute-start.4
  61.8 1.9 %collective-permute-start.9 = (bf16[1,128,128]{2,1,0:T(8,128)(2,1)S(1)}, bf16[1,128,128]{2,1,0:T(8,128)(2,1)S(1)}, u32[]{:S(2)}, u32[]{:S(2)}) collective-permute-start(bf16[1,128,128]{2,1,0:T(8,128)(2,1)S(1)} %get-tuple-element.10), channel_id=1, source_target_pairs={{16,3},{96,9},{17,16},{97,26},{18,33},{98,43},{19,50},{99,56},{20,... | collective-permute-start | bytes 98312 | tf_op jit(solution)/shard_map/ppermute | solution.py:244
  63.7 6.3 %collective-permute-done.9.far = bf16[1,128,128]{2,1,0:T(8,128)(2,1)S(1)} collective-permute-done((bf16[1,128,128]{2,1,0:T(8,128)(2,1)S(1)}, bf16[1,128,128]{2,1,0:T(8,128)(2,1)S(1)}, u32[]{:S(2)}, u32[]{:S(2)}) %collective-permute-start.9) | collective-permute-done | bytes 32800 | tf_op jit(solution)/shard_map/ppermute | solution.py:244
  70.0 1.3 %collective-permute-start.8 = (bf16[2,128,128]{2,1,0:T(8,128)(2,1)S(1)}, bf16[2,128,128]{2,1,0:T(8,128)(2,1)S(1)}, u32[]{:S(2)}, u32[]{:S(2)}) collective-permute-start(bf16[2,128,128]{2,1,0:T(8,128)(2,1)S(1)} %get-tuple-element.9), channel_id=1, source_target_pairs={{0,3},{112,9},{1,16},{113,26},{2,33},{114,43},{3,50},{115,56},{4,7... | collective-permute-start | bytes 196616 | tf_op jit(solution)/shard_map/ppermute | solution.py:243
  71.3 8.8 %collective-permute-done.8.near = bf16[2,128,128]{2,1,0:T(8,128)(2,1)S(1)} collective-permute-done((bf16[2,128,128]{2,1,0:T(8,128)(2,1)S(1)}, bf16[2,128,128]{2,1,0:T(8,128)(2,1)S(1)}, u32[]{:S(2)}, u32[]{:S(2)}) %collective-permute-start.8) | collective-permute-done | bytes 65568 | tf_op jit(solution)/shard_map/ppermute | solution.py:243
  80.1 0.0 collective-permute-done.7.r3
  80.1 0.0 collective-permute-done.6.r2
  80.1 0.0 collective-permute-done.5.r1
  80.1 0.0 collective-permute-done.4.r0
  80.2 1.1 %shard_map.50 = bf16[512,1024]{1,0:T(8,128)(2,1)} custom-call(bf16[5,128,128]{2,1,0:T(8,128)(2,1)S(1)} %collective-permute-done.4.r0, bf16[5,128,128]{2,1,0:T(8,128)(2,1)S(1)} %collective-permute-done.5.r1, bf16[5,128,128]{2,1,0:T(8,128)(2,1)S(1)} %collective-permute-done.6.r2, bf16[5,128,128]{2,1,0:T(8,128)(2,1)S(1)} %collective-permute-done.7.r3, ...), custom_call_target="tpu_custom_call" | custom-call | tf_op jit(solution)/shard_map/pallas_call | solution.py:246
  (1 shorter events, 0.0 us)
Async XLA Ops:
  0.0 0.7 copy-start.3
  0.7 1.2 %copy-start = (bf16[512,1024]{1,0:T(8,128)(2,1)S(1)}, bf16[512,1024]{1,0:T(8,128)(2,1)}, u32[]{:S(2)}) copy-start(bf16[512,1024]{1,0:T(8,128)(2,1)} %param.4) | copy-start | bytes 3145732
  2.8 15.1 %copy-start.1 = (s32[64,64]{1,0:T(8,128)S(1)}, s32[64,64]{1,0:T(8,128)}, u32[]{:S(2)}) copy-start(s32[64,64]{1,0:T(8,128)} %pattern.2) | copy-start | bytes 49156
  14.6 3.2 %collective-permute-start = (bf16[8,12,16,128]{3,2,1,0:T(8,128)(2,1)S(1)}, bf16[8,12,16,128]{3,2,1,0:T(8,128)(2,1)S(1)}, u32[]{:S(2)}, u32[]{:S(2)}) collective-permute-start(bf16[8,12,16,128]{3,2,1,0:T(8,128)(2,1)S(1)} %all_to_all.10.mine), channel_id=1, source_target_pairs={{0,8},{8,0},{1,9},{9,1},{2,10},{10,2},{3,11},{11,3},{4,12},{12,4},... | collective-permute-start | bytes 1179656 | tf_op jit(solution)/shard_map/ppermute | solution.py:214
  19.4 4.2 %collective-permute-start.2 = (bf16[5,16,128]{2,1,0:T(8,128)(2,1)S(1)}, bf16[5,16,128]{2,1,0:T(8,128)(2,1)S(1)}, u32[]{:S(2)}, u32[]{:S(2)}) collective-permute-start(bf16[5,16,128]{2,1,0:T(8,128)(2,1)S(1)} %get-tuple-element.11), channel_id=1, source_target_pairs={{1,0},{2,1},{3,2},{0,3},{5,4},{6,5},{7,6},{4,7},{9,8},{10,9},{11,1... | collective-permute-start | bytes 61448 | tf_op jit(solution)/shard_map/ppermute | solution.py:234
  22.0 5.0 %collective-permute-start.1 = (bf16[5,16,128]{2,1,0:T(8,128)(2,1)S(1)}, bf16[5,16,128]{2,1,0:T(8,128)(2,1)S(1)}, u32[]{:S(2)}, u32[]{:S(2)}) collective-permute-start(bf16[5,16,128]{2,1,0:T(8,128)(2,1)S(1)} %get-tuple-element.12), channel_id=1, source_target_pairs={{0,1},{1,2},{2,3},{3,0},{4,5},{5,6},{6,7},{7,4},{8,9},{9,10},{10,1... | collective-permute-start | bytes 61448 | tf_op jit(solution)/shard_map/ppermute | solution.py:233
  27.2 23.7 %copy-start.2 = (s32[64,64]{1,0:T(8,128)S(1)}, s32[64,64]{1,0:T(8,128)}, u32[]{:S(2)}) copy-start(s32[64,64]{1,0:T(8,128)} %pattern.3) | copy-start | bytes 49156
  46.0 4.9 %collective-permute-start.3 = (bf16[16,13,16,128]{3,2,1,0:T(8,128)(2,1)S(1)}, bf16[16,13,16,128]{3,2,1,0:T(8,128)(2,1)S(1)}, u32[]{:S(2)}, u32[]{:S(2)}) collective-permute-start(bf16[16,13,16,128]{3,2,1,0:T(8,128)(2,1)S(1)} %all_to_all.11.mine), channel_id=1, source_target_pairs={{0,8},{8,0},{1,9},{9,1},{2,10},{10,2},{3,11},{11,3},{4,12},{12,4},... | collective-permute-start | bytes 2555912 | tf_op jit(solution)/shard_map/ppermute | solution.py:214
  52.8 27.4 %collective-permute-start.7 = (bf16[5,128,128]{2,1,0:T(8,128)(2,1)S(1)}, bf16[5,128,128]{2,1,0:T(8,128)(2,1)S(1)}, u32[]{:S(2)}, u32[]{:S(2)}) collective-permute-start(bf16[5,128,128]{2,1,0:T(8,128)(2,1)S(1)} %get-tuple-element.8), channel_id=1, source_target_pairs={{48,0},{112,8},{49,17},{113,25},{50,34},{114,42},{51,51},{115,59},... | collective-permute-start | bytes 491528 | tf_op jit(solution)/shard_map/ppermute | solution.py:245
  53.5 26.7 %collective-permute-start.6 = (bf16[5,128,128]{2,1,0:T(8,128)(2,1)S(1)}, bf16[5,128,128]{2,1,0:T(8,128)(2,1)S(1)}, u32[]{:S(2)}, u32[]{:S(2)}) collective-permute-start(bf16[5,128,128]{2,1,0:T(8,128)(2,1)S(1)} %get-tuple-element.8), channel_id=1, source_target_pairs={{32,0},{96,8},{33,17},{97,25},{34,34},{98,42},{35,51},{99,59},{36,... | collective-permute-start | bytes 491528 | tf_op jit(solution)/shard_map/ppermute | solution.py:245
  54.1 26.0 %collective-permute-start.5 = (bf16[5,128,128]{2,1,0:T(8,128)(2,1)S(1)}, bf16[5,128,128]{2,1,0:T(8,128)(2,1)S(1)}, u32[]{:S(2)}, u32[]{:S(2)}) collective-permute-start(bf16[5,128,128]{2,1,0:T(8,128)(2,1)S(1)} %get-tuple-element.8), channel_id=1, source_target_pairs={{16,0},{80,8},{17,17},{81,25},{18,34},{82,42},{19,51},{83,59},{20,... | collective-permute-start | bytes 491528 | tf_op jit(solution)/shard_map/ppermute | solution.py:245
  61.1 19.0 %collective-permute-start.4 = (bf16[5,128,128]{2,1,0:T(8,128)(2,1)S(1)}, bf16[5,128,128]{2,1,0:T(8,128)(2,1)S(1)}, u32[]{:S(2)}, u32[]{:S(2)}) collective-permute-start(bf16[5,128,128]{2,1,0:T(8,128)(2,1)S(1)} %get-tuple-element.8), channel_id=1, source_target_pairs={{0,0},{64,8},{1,17},{65,25},{2,34},{66,42},{3,51},{67,59},{4,4},{6... | collective-permute-start | bytes 491528 | tf_op jit(solution)/shard_map/ppermute | solution.py:245
  61.8 8.2 %collective-permute-start.9 = (bf16[1,128,128]{2,1,0:T(8,128)(2,1)S(1)}, bf16[1,128,128]{2,1,0:T(8,128)(2,1)S(1)}, u32[]{:S(2)}, u32[]{:S(2)}) collective-permute-start(bf16[1,128,128]{2,1,0:T(8,128)(2,1)S(1)} %get-tuple-element.10), channel_id=1, source_target_pairs={{16,3},{96,9},{17,16},{97,26},{18,33},{98,43},{19,50},{99,56},{20,... | collective-permute-start | bytes 98312 | tf_op jit(solution)/shard_map/ppermute | solution.py:244
  70.0 10.1 %collective-permute-start.8 = (bf16[2,128,128]{2,1,0:T(8,128)(2,1)S(1)}, bf16[2,128,128]{2,1,0:T(8,128)(2,1)S(1)}, u32[]{:S(2)}, u32[]{:S(2)}) collective-permute-start(bf16[2,128,128]{2,1,0:T(8,128)(2,1)S(1)} %get-tuple-element.9), channel_id=1, source_target_pairs={{0,3},{112,9},{1,16},{113,26},{2,33},{114,43},{3,50},{115,56},{4,7... | collective-permute-start | bytes 196616 | tf_op jit(solution)/shard_map/ppermute | solution.py:243

commit v2 on v0

v2 whole, which is shorter than its diff:
```python
import functools

import jax
import jax.numpy as jnp
import numpy as np
from jax import lax
from jax.experimental import pallas as pl
from jax.experimental.pallas import tpu as pltpu
from jax.sharding import Mesh
from jax.sharding import PartitionSpec as P

BS = 128
GRID = (4, 2, 2, 2, 2, 2)
AXES = ("x", "zl", "core", "yh", "yl", "zh")
ROW = ("x", "zl", "core")
COL = ("yh", "yl", "zh")
CHIPS = 8
PART = BS // CHIPS
WIDE = 34
WIN = 28
STARTS = (3, 6, 3, 0)

VMEM = pl.BlockSpec(memory_space=pltpu.VMEM)
SMEM = pl.BlockSpec(memory_space=pltpu.SMEM)
HBM = pl.BlockSpec(memory_space=pltpu.HBM)
PARAMS = pltpu.CompilerParams(vmem_limit_bytes=48 * 1024 * 1024)


def chip_index():
    return lax.axis_index("x") * 2 + lax.axis_index("zl")


def group_index():
    return lax.axis_index("yl") * 2 + lax.axis_index("zh")


def pick_kernel(order, built, out, order_s, built_v, sem):
    copies = [
        pltpu.make_async_copy(order, order_s, sem.at[0]),
        pltpu.make_async_copy(built, built_v, sem.at[1]),
    ]
    for copy in copies:
        copy.start()
    for copy in copies:
        copy.wait()
    first = (chip_index() * 2 + lax.axis_index("core")) * 4
    zh = lax.axis_index("zh")
    for k in range(4):
        row = order_s[first + k]
        for d in range(3):
            col = lax.rem(row + d + 31, 8)
            at = pl.ds(pl.multiple_of(col * BS, BS), BS)
            for chip in range(0, CHIPS, 2):
                out[chip, 3 * k + d] = built_v[k, chip + zh, :, at]
                out[chip + 1, 3 * k + d] = built_v[k, chip + 1 - zh, :, at]


def place_kernel(order, pattern, mine, other, out, inverse):
    for k in range(64):
        inverse[order[k]] = k
    core = lax.axis_index("core")
    yh = lax.axis_index("yh")
    base = group_index() * 8
    for bl in range(8):
        for e in range(3):
            row = lax.rem(base + bl + e + 31, 32) + 32 * core
            at = inverse[row]
            device = at // 4
            slot = lax.rem(at, 4) * 3 + (2 - e)
            chip = device // 2
            here = lax.rem(device, 2) == core
            keep = pattern[row, base + bl + 32 * yh] != 0
            value = jnp.where(here, mine[chip, slot], other[chip, slot])
            out[3 * bl + e] = jnp.where(keep, value, jnp.zeros_like(value))


def distance(chip):
    return lax.rem(chip - group_index() + 8, 4)


def window_kernel(left, own, right, out, wide):
    wide[:5] = left[...]
    wide[5:29] = own[...]
    wide[29:] = right[...]
    for chip in range(CHIPS):
        away = distance(chip)
        start = jnp.where(away == 1, STARTS[1], jnp.where(away == 3, STARTS[3], STARTS[0]))
        value = wide[pl.ds(start, WIN)]
        for half in range(2):
            out[2 * chip + half] = value


def purify_kernel(pattern, mine, other, out, squares, rounded):
    core = lax.axis_index("core")
    yh = lax.axis_index("yh")
    zh = lax.axis_index("zh")
    chip = chip_index()
    away = distance(chip)
    row_half = chip // 4
    base = group_index() * 8
    out[...] = jnp.zeros_like(out)

    def dot(a, b):
        return jnp.dot(a, b, preferred_element_type=jnp.float32)

    def block(ref, n, half):
        rows = [ref[2 * (p + zh if p % 2 == 0 else p - zh) + half, n] for p in range(CHIPS)]
        return jnp.concatenate(rows, 0)

    def kept(row, col, half):
        i = lax.rem(base + row + 32, 32) + 32 * row_half
        j = lax.rem(base + col + 32, 32) + 32 * half
        return pattern[i, j] != 0

    def work(u, start, rows, results):
        halves = (mine, other) if u == 0 else (other, mine)
        same = row_half == u

        def number(row, col):
            return 2 * col + row + 6 - start

        def column(row, col, half):
            return jnp.concatenate([block(h, number(row, col), half) for h in halves], 0)

        def whole(row, col):
            return jnp.concatenate([column(row, col, half) for half in range(2)], 1)

        def left(row, col):
            n = number(row, col)
            parts = [
                jnp.where(same, block(mine, n, half), block(other, n, half)) for half in range(2)
            ]
            return jnp.concatenate(parts, 1)

        near = lambda a, b, d=1: abs(a - b) <= d
        span = range(-2, 10)
        cols = {a: sorted({k for b, j in results if b == a for k in span if near(k, j) and near(k, a, 2)}) for a in rows}
        for a in rows:
            for k in cols[a]:
                ls = [l for l in span if near(l, a) and near(l, k)]
                total = dot(
                    jnp.concatenate([left(a, l) for l in ls], 1),
                    jnp.concatenate([whole(l, k) for l in ls], 0),
                )
                at = (rows.index(a), k - cols[a][0])
                parts = []
                for half in range(2):
                    part = total[:, half * BS : (half + 1) * BS]
                    parts.append(jnp.where(kept(a, k, half), part, jnp.zeros_like(part)))
                squares[at] = jnp.where(yh == 0, parts[0], parts[1])
                rounded[at] = jnp.concatenate(parts, 1).astype(jnp.bfloat16)
        for (a, j), (r, c) in results.items():
            ks = [k for k in cols[a] if near(k, j)]
            r_at, first = rows.index(a), cols[a][0]
            total = dot(
                jnp.concatenate([rounded[r_at, k - first] for k in ks], 1),
                jnp.concatenate([column(k, j, yh) for k in ks], 0),
            )
            value = 3.0 * squares[r_at, j - first] - 2.0 * total
            value = jnp.where(kept(a, j, yh), value, jnp.zeros_like(value))
            out[r * BS : (r + 1) * BS, c * BS : (c + 1) * BS] = value.astype(jnp.bfloat16)

    for u in range(2):

        @pl.when(jnp.logical_and(away == 0, core == u))
        def _(u=u):
            rows = list(range(4 * u, 4 * u + 4))
            spots = [(a, j) for a in rows for j in range(a - 2, a + 3) if 0 <= j < 8]
            work(u, STARTS[0], rows, {(a, j): (a - 4 * u, j) for a, j in spots})

    @pl.when(jnp.logical_and(away == 1, core == 0))
    def _():
        work(0, STARTS[1], [8, 9], {(8, 6): (0, 6), (8, 7): (0, 7), (9, 7): (1, 7)})

    @pl.when(jnp.logical_and(away == 3, core == 1))
    def _():
        work(1, STARTS[3], [-1, -2], {(-1, 1): (3, 1), (-1, 0): (3, 0), (-2, 0): (2, 0)})


def to_group(step):
    return [
        (
            ((zl * 2 + g // 2) * 2) + g % 2,
            (((1 - zl) * 2 + (g + step) % 4 // 2) * 2) + (g + step) % 2,
        )
        for zl in range(2)
        for g in range(4)
    ]


def call(kernel, shape, specs, out_spec=VMEM, scratch=()):
    make = lambda s: jax.ShapeDtypeStruct(s, jnp.bfloat16)
    many = isinstance(shape, list)
    return pl.pallas_call(
        kernel,
        out_shape=[make(s) for s in shape] if many else make(shape),
        in_specs=specs,
        out_specs=[out_spec] * len(shape) if many else out_spec,
        scratch_shapes=list(scratch),
        compiler_params=PARAMS,
    )


def in_hbm(a):
    return pltpu.with_memory_space_constraint(a, pltpu.HBM)


def swap_cores(a):
    return lax.ppermute(a, "core", [(0, 1), (1, 0)])


def body(built, build_order, p_pattern, q_pattern):
    parts = call(
        pick_kernel,
        (CHIPS, 12, PART, BS),
        [HBM, HBM],
        scratch=[
            pltpu.SMEM((64,), jnp.int32),
            pltpu.VMEM((4, CHIPS, PART, 8 * BS), jnp.bfloat16),
            pltpu.SemaphoreType.DMA((2,)),
        ],
    )(in_hbm(build_order), in_hbm(built.reshape(4, CHIPS, PART, 8 * BS)))
    parts = lax.all_to_all(parts, ("x", "zl"), 0, 0, tiled=True)
    placed = call(
        place_kernel,
        (24, PART, BS),
        [SMEM, SMEM, VMEM, VMEM],
        scratch=[pltpu.SMEM((64,), jnp.int32)],
    )(build_order, p_pattern, parts, swap_cores(parts))
    left = lax.ppermute(placed[19:], ("zl", "yl", "zh"), to_group(1))
    right = lax.ppermute(placed[:5], ("zl", "yl", "zh"), to_group(3))
    windows = call(
        window_kernel,
        (2 * CHIPS, WIN, PART, BS),
        [VMEM] * 3,
        scratch=[pltpu.VMEM((WIDE, PART, BS), jnp.bfloat16)],
    )(left, placed, right)
    windows = lax.all_to_all(windows, ("x", "zl", "yh"), 0, 0, tiled=True)
    return call(
        purify_kernel,
        (4 * BS, 8 * BS),
        [SMEM, VMEM, VMEM],
        scratch=[
            pltpu.VMEM((4, 5, BS, BS), jnp.float32),
            pltpu.VMEM((4, 5, BS, 2 * BS), jnp.bfloat16),
        ],
    )(q_pattern, windows, swap_cores(windows))


def solution(mesh):
    fine = Mesh(mesh.devices.reshape(GRID), AXES)
    placed = (P(ROW, COL), P(), P(), P())
    return jax.shard_map(
        body, mesh=fine, in_specs=placed, out_specs=P(ROW, COL), check_vma=False
    )
```

time: 388 us -> 68.2 us (0.18)
  waiting for transfers between devices: 310 us -> 9.5 us
  blocking collectives: 0 us -> 41.6 us
  matrix products: 32.4 us -> 0 us
  local copies, waits for them, and re-layouts: 22.4 us -> 0.02 us
  between operations: 13.2 us -> 0.05 us
  starting transfers between devices: 0.08 us -> 9.74 us
  other arithmetic: 8.79 us -> 0 us
  Pallas kernels: 0 us -> 6.98 us
    all_gather x3 -> x0, waiting for transfers between devices: 310 us -> none  [the longest x1 108 us: body(): lax.all_gather(local_tile, 'col', axis=1, tiled=True)]
    all_to_all x0 -> x2, blocking collectives: none -> 41.6 us  [the longest x1 28.5 us: body(): windows = lax.all_to_all(windows, ('x', 'zl', 'yh'), 0, 0, tiled=True)]
    dot_general x2 -> x0, matrix products: 32.4 us -> none  [contract(): return jnp.dot(portion, col_panel, preferred_element_type=jnp.float32)]
    gather x1 -> x0, local copies, waits for them, and re-layouts: 13.4 us -> none  [body(): ordered = blocks[inverse].reshape(block_count, BS, col_count, BS)]
    ppermute x0 -> x4, starting transfers between devices: none -> 9.74 us  [the longest x2 5.79 us: swap_cores(): return lax.ppermute(a, 'core', [(0, 1), (1, 0)])]
    ppermute x0 -> x4, waiting for transfers between devices: none -> 9.5 us  [the longest x2 4.76 us: swap_cores(): return lax.ppermute(a, 'core', [(0, 1), (1, 0)])]
    pallas_call x0 -> x4, Pallas kernels: none -> 6.98 us  [the longest x1 3.87 us: body(): call(purify_kernel, (4 * BS, 8 * BS), [SMEM, VMEM, VMEM], scratch=[pltpu....]
    mul x1 -> x0, other arithmetic: 6.51 us -> none  [body(): ordered * col_mask[:, None, :, None]]
  transfers between devices with their start and end apart: 3 -> 4, of which waited for: 3 -> 4; matrix products, arithmetic and copies ran while one was open for 1% -> 0% of each run, Pallas kernels for 0% -> 0%
where the time goes in v2:
time: 68.2 us; the launch traced here: 67.9 us
  blocking collectives  41.6 us (61%)
  starting transfers between devices  9.74 us (14%)
  waiting for transfers between devices  9.5 us (14%)
  Pallas kernels  6.98 us (10%)
    all_to_all x1, blocking collectives, body(): windows = lax.all_to_all(windows, ('x', 'zl', 'yh'), 0, 0, tiled=True)  28.5 us
    all_to_all x1, blocking collectives, body(): parts = lax.all_to_all(parts, ('x', 'zl'), 0, 0, tiled=True)  13.2 us
    ppermute x2, starting transfers between devices, swap_cores(): return lax.ppermute(a, 'core', [(0, 1), (1, 0)])  5.79 us
    ppermute x2, waiting for transfers between devices, swap_cores(): return lax.ppermute(a, 'core', [(0, 1), (1, 0)])  4.76 us
    ppermute x1, starting transfers between devices, body(): right = lax.ppermute(placed[:5], ('zl', 'yl', 'zh'), to_group(3))  3.95 us
    pallas_call x1, Pallas kernels, body(): call(purify_kernel, (4 * BS, 8 * BS), [SMEM, VMEM, VMEM], scratch=[pltpu....  3.87 us
    ppermute x1, waiting for transfers between devices, body(): left = lax.ppermute(placed[19:], ('zl', 'yl', 'zh'), to_group(1))  3.83 us
    pallas_call x1, Pallas kernels, body(): call(place_kernel, (24, PART, BS), [SMEM, SMEM, VMEM, VMEM], scratch=[plt...  1.49 us
  transfers between devices with their start and end apart: 4, of which 4 were waited for; matrix products, arithmetic and copies ran while one was open for 0% of the time, Pallas kernels for 0%

profile of v2, /device:TPU:1, one launch (start us, length us, event | category | flops | bytes accessed | tf_op | source)
XLA Modules:
  0.0 67.9 jit_solution(5634335074416037368)
XLA Ops:
  0.0 0.0 copy-start.2
  0.0 0.0 copy-start.1
  0.0 1.4 %shard_map.46 = bf16[8,12,16,128]{3,2,1,0:T(8,128)(2,1)S(1)} custom-call(s32[64]{0:T(128)} %order.3, bf16[4,8,16,1024]{3,2,1,0:T(8,128)(2,1)} %bitcast.1), custom_call_target="tpu_custom_call" | custom-call | tf_op jit(solution)/shard_map/pallas_call | solution.py:213
  1.4 13.2 %all_to_all.10.mine = bf16[8,12,16,128]{3,2,1,0:T(8,128)(2,1)S(1)} all-to-all(bf16[8,12,16,128]{3,2,1,0:T(8,128)(2,1)S(1)} %shard_map.46), channel_id=1, replica_groups=mesh['x'=4,'zl'=2,'core'=2,'yh'=2,'yl'=2,'zh'=2] {'x','zl'}, dimensions={0} | all-to-all | bytes 786432 | tf_op jit(solution)/shard_map/all_to_all | solution.py:223
  14.5 2.3 %collective-permute-start = (bf16[8,12,16,128]{3,2,1,0:T(8,128)(2,1)S(1)}, bf16[8,12,16,128]{3,2,1,0:T(8,128)(2,1)S(1)}, u32[]{:S(2)}, u32[]{:S(2)}) collective-permute-start(bf16[8,12,16,128]{3,2,1,0:T(8,128)(2,1)S(1)} %all_to_all.10.mine), channel_id=1, source_target_pairs={{0,8},{8,0},{1,9},{9,1},{2,10},{10,2},{3,11},{11,3},{4,12},{12,4},... | collective-permute-start | bytes 1179656 | tf_op jit(solution)/shard_map/ppermute | solution.py:209
  16.8 1.3 %collective-permute-done.other = bf16[8,12,16,128]{3,2,1,0:T(8,128)(2,1)S(1)} collective-permute-done((bf16[8,12,16,128]{3,2,1,0:T(8,128)(2,1)S(1)}, bf16[8,12,16,128]{3,2,1,0:T(8,128)(2,1)S(1)}, u32[]{:S(2)}, u32[]{:S(2)}) %collective-permute-start) | collective-permute-done | bytes 393248 | tf_op jit(solution)/shard_map/ppermute | solution.py:209
  18.2 0.0 copy-done.2
  18.2 0.0 copy-done.1
  18.2 1.5 %shard_map.47.own = bf16[24,16,128]{2,1,0:T(8,128)(2,1)S(1)} custom-call(s32[64]{0:T(128)S(1)} %copy-done.2, s32[64,64]{1,0:T(8,128)S(1)} %copy-done.1, bf16[8,12,16,128]{3,2,1,0:T(8,128)(2,1)S(1)} %all_to_all.10.mine, bf16[8,12,16,128]{3,2,1,0:T(8,128)(2,1)S(1)} %collective-permute-done.other), custom_call_target="tpu_custom_call" | custom-call | tf_op jit(solution)/shard_map/pallas_call | solution.py:224
  19.7 4.0 %collective-permute-start.2 = (bf16[5,16,128]{2,1,0:T(8,128)(2,1)S(1)}, bf16[5,16,128]{2,1,0:T(8,128)(2,1)S(1)}, u32[]{:S(2)}, u32[]{:S(2)}) collective-permute-start(bf16[5,16,128]{2,1,0:T(8,128)(2,1)S(1)} %get-tuple-element.5), channel_id=1, source_target_pairs={{0,19},{1,16},{2,17},{3,18},{16,3},{17,0},{18,1},{19,2},{4,23},{5,... | collective-permute-start | bytes 61448 | tf_op jit(solution)/shard_map/ppermute | solution.py:231
  23.7 0.0 collective-permute-start.1
  23.7 0.9 %collective-permute-done.2.right = bf16[5,16,128]{2,1,0:T(8,128)(2,1)S(1)} collective-permute-done((bf16[5,16,128]{2,1,0:T(8,128)(2,1)S(1)}, bf16[5,16,128]{2,1,0:T(8,128)(2,1)S(1)}, u32[]{:S(2)}, u32[]{:S(2)}) %collective-permute-start.2) | collective-permute-done | bytes 20512 | tf_op jit(solution)/shard_map/ppermute | solution.py:231
  24.6 3.8 %collective-permute-done.1.left = bf16[5,16,128]{2,1,0:T(8,128)(2,1)S(1)} collective-permute-done((bf16[5,16,128]{2,1,0:T(8,128)(2,1)S(1)}, bf16[5,16,128]{2,1,0:T(8,128)(2,1)S(1)}, u32[]{:S(2)}, u32[]{:S(2)}) %collective-permute-start.1) | collective-permute-done | bytes 20512 | tf_op jit(solution)/shard_map/ppermute | solution.py:230
  28.4 0.3 shard_map.48
  28.7 0.0 copy-start
  28.7 28.5 %all_to_all.11.mine = bf16[16,28,16,128]{3,2,1,0:T(8,128)(2,1)S(1)} all-to-all(bf16[16,28,16,128]{3,2,1,0:T(8,128)(2,1)S(1)} %shard_map.48), channel_id=1, replica_groups=mesh['x'=4,'zl'=2,'core'=2,'yh'=2,'yl'=2,'zh'=2] {'x','zl','yh'}, dimensions={0} | all-to-all | bytes 3670016 | tf_op jit(solution)/shard_map/all_to_all | solution.py:238
  57.1 3.5 %collective-permute-start.3 = (bf16[16,28,16,128]{3,2,1,0:T(8,128)(2,1)S(1)}, bf16[16,28,16,128]{3,2,1,0:T(8,128)(2,1)S(1)}, u32[]{:S(2)}, u32[]{:S(2)}) collective-permute-start(bf16[16,28,16,128]{3,2,1,0:T(8,128)(2,1)S(1)} %all_to_all.11.mine), channel_id=1, source_target_pairs={{0,8},{8,0},{1,9},{9,1},{2,10},{10,2},{3,11},{11,3},{4,12},{12,4},... | collective-permute-start | bytes 5505032 | tf_op jit(solution)/shard_map/ppermute | solution.py:209
  60.6 3.4 %collective-permute-done.3.other = bf16[16,28,16,128]{3,2,1,0:T(8,128)(2,1)S(1)} collective-permute-done((bf16[16,28,16,128]{3,2,1,0:T(8,128)(2,1)S(1)}, bf16[16,28,16,128]{3,2,1,0:T(8,128)(2,1)S(1)}, u32[]{:S(2)}, u32[]{:S(2)}) %collective-permute-start.3) | collective-permute-done | bytes 1835040 | tf_op jit(solution)/shard_map/ppermute | solution.py:209
  64.0 0.0 copy-done
  64.0 3.9 %shard_map.49 = bf16[512,1024]{1,0:T(8,128)(2,1)} custom-call(s32[64,64]{1,0:T(8,128)S(1)} %copy-done, bf16[16,28,16,128]{3,2,1,0:T(8,128)(2,1)S(1)} %all_to_all.11.mine, bf16[16,28,16,128]{3,2,1,0:T(8,128)(2,1)S(1)} %collective-permute-done.3.other), custom_call_target="tpu_custom_call" | custom-call | tf_op jit(solution)/shard_map/pallas_call | solution.py:239
  (1 shorter events, 0.0 us)
Async XLA Ops:
  0.0 18.2 %copy-start.2 = (s32[64]{0:T(128)S(1)}, s32[64]{0:T(128)}, u32[]{:S(2)}) copy-start(s32[64]{0:T(128)} %order.3) | copy-start | bytes 772
  0.0 18.2 %copy-start.1 = (s32[64,64]{1,0:T(8,128)S(1)}, s32[64,64]{1,0:T(8,128)}, u32[]{:S(2)}) copy-start(s32[64,64]{1,0:T(8,128)} %pattern.2) | copy-start | bytes 49156
  14.5 3.6 %collective-permute-start = (bf16[8,12,16,128]{3,2,1,0:T(8,128)(2,1)S(1)}, bf16[8,12,16,128]{3,2,1,0:T(8,128)(2,1)S(1)}, u32[]{:S(2)}, u32[]{:S(2)}) collective-permute-start(bf16[8,12,16,128]{3,2,1,0:T(8,128)(2,1)S(1)} %all_to_all.10.mine), channel_id=1, source_target_pairs={{0,8},{8,0},{1,9},{9,1},{2,10},{10,2},{3,11},{11,3},{4,12},{12,4},... | collective-permute-start | bytes 1179656 | tf_op jit(solution)/shard_map/ppermute | solution.py:209
  19.7 4.9 %collective-permute-start.2 = (bf16[5,16,128]{2,1,0:T(8,128)(2,1)S(1)}, bf16[5,16,128]{2,1,0:T(8,128)(2,1)S(1)}, u32[]{:S(2)}, u32[]{:S(2)}) collective-permute-start(bf16[5,16,128]{2,1,0:T(8,128)(2,1)S(1)} %get-tuple-element.5), channel_id=1, source_target_pairs={{0,19},{1,16},{2,17},{3,18},{16,3},{17,0},{18,1},{19,2},{4,23},{5,... | collective-permute-start | bytes 61448 | tf_op jit(solution)/shard_map/ppermute | solution.py:231
  23.7 4.7 %collective-permute-start.1 = (bf16[5,16,128]{2,1,0:T(8,128)(2,1)S(1)}, bf16[5,16,128]{2,1,0:T(8,128)(2,1)S(1)}, u32[]{:S(2)}, u32[]{:S(2)}) collective-permute-start(bf16[5,16,128]{2,1,0:T(8,128)(2,1)S(1)} %get-tuple-element.6), channel_id=1, source_target_pairs={{0,17},{1,18},{2,19},{3,16},{16,1},{17,2},{18,3},{19,0},{4,21},{5,... | collective-permute-start | bytes 61448 | tf_op jit(solution)/shard_map/ppermute | solution.py:230
  28.7 35.4 %copy-start = (s32[64,64]{1,0:T(8,128)S(1)}, s32[64,64]{1,0:T(8,128)}, u32[]{:S(2)}) copy-start(s32[64,64]{1,0:T(8,128)} %pattern.3) | copy-start | bytes 49156
  57.1 6.9 %collective-permute-start.3 = (bf16[16,28,16,128]{3,2,1,0:T(8,128)(2,1)S(1)}, bf16[16,28,16,128]{3,2,1,0:T(8,128)(2,1)S(1)}, u32[]{:S(2)}, u32[]{:S(2)}) collective-permute-start(bf16[16,28,16,128]{3,2,1,0:T(8,128)(2,1)S(1)} %all_to_all.11.mine), channel_id=1, source_target_pairs={{0,8},{8,0},{1,9},{9,1},{2,10},{10,2},{3,11},{11,3},{4,12},{12,4},... | collective-permute-start | bytes 5505032 | tf_op jit(solution)/shard_map/ppermute | solution.py:209

commit v3 on v2

v3 whole, which is shorter than its diff:
```python
import functools

import jax
import jax.numpy as jnp
import numpy as np
from jax import lax
from jax.experimental import pallas as pl
from jax.experimental.pallas import tpu as pltpu
from jax.sharding import Mesh
from jax.sharding import PartitionSpec as P

BS = 128
GRID = (4, 2, 2, 2, 2, 2)
AXES = ("x", "zl", "core", "yh", "yl", "zh")
ROW = ("x", "zl", "core")
COL = ("yh", "yl", "zh")
CHIPS = 8
PART = BS // CHIPS
PARTS = CHIPS * 12
WIDE = 34
WIN = 28
STARTS = (3, 6, 3, 0)

VMEM = pl.BlockSpec(memory_space=pltpu.VMEM)
SMEM = pl.BlockSpec(memory_space=pltpu.SMEM)
ANY = pl.BlockSpec(memory_space=pl.ANY)
HBM = pl.BlockSpec(memory_space=pltpu.HBM)
PARAMS = pltpu.CompilerParams(vmem_limit_bytes=48 * 1024 * 1024)


def chip_index():
    return lax.axis_index("x") * 2 + lax.axis_index("zl")


def group_index():
    return lax.axis_index("yl") * 2 + lax.axis_index("zh")


def pick_kernel(order, built, out, order_s, built_v, sem):
    copies = [
        pltpu.make_async_copy(order, order_s, sem.at[0]),
        pltpu.make_async_copy(built, built_v, sem.at[1]),
    ]
    for copy in copies:
        copy.start()
    for copy in copies:
        copy.wait()
    first = (chip_index() * 2 + lax.axis_index("core")) * 4
    zh = lax.axis_index("zh")
    for k in range(4):
        row = order_s[first + k]
        for d in range(3):
            col = lax.rem(row + d + 31, 8)
            at = pl.ds(pl.multiple_of(col * BS, BS), BS)
            for chip in range(0, CHIPS, 2):
                out[chip, 3 * k + d] = built_v[k, chip + zh, :, at]
                out[chip + 1, 3 * k + d] = built_v[k, chip + 1 - zh, :, at]


def find_kernel(order_in, pattern_in, ready, out, order, pattern, inverse, sem):
    core = lax.axis_index("core")
    yh = lax.axis_index("yh")
    base = group_index() * 8
    copies = [pltpu.make_async_copy(order_in, order, sem.at[0])]
    for n in range(3):
        rows = lax.rem(base + 8 * n + 24, 32) + 32 * core
        copies.append(
            pltpu.make_async_copy(
                pattern_in.at[pl.ds(pl.multiple_of(rows, 8), 8)],
                pattern.at[pl.ds(8 * n, 8)],
                sem.at[1 + n],
            )
        )
    for copy in copies:
        copy.start()
    copies[0].wait()
    for k in range(64):
        inverse[order[k]] = k
    for copy in copies[1:]:
        copy.wait()
    for bl in range(8):
        for e in range(3):
            row = lax.rem(base + bl + e + 31, 32) + 32 * core
            at = inverse[row]
            device = at // 4
            slot = (device // 2) * 12 + lax.rem(at, 4) * 3 + (2 - e)
            slot = jnp.where(lax.rem(device, 2) == core, slot, slot + PARTS)
            keep = pattern[7 + bl + e, base + bl + 32 * yh] != 0
            out[3 * bl + e] = jnp.where(keep, slot, 2 * PARTS)


def take(found, mine, other, n):
    at = found[n]
    here = at < PARTS
    at_mine = jnp.where(here, at, 0)
    at_other = jnp.where(jnp.logical_and(at >= PARTS, at < 2 * PARTS), at - PARTS, 0)
    value = jnp.where(here, mine[at_mine], other[at_other])
    return jnp.where(at < 2 * PARTS, value, jnp.zeros_like(value))


def edge_kernel(found, mine, other, first, last):
    for n in range(5):
        first[n] = take(found, mine, other, n)
        last[n] = take(found, mine, other, 19 + n)


def inner_kernel(found, mine, other, out):
    for n in range(14):
        out[n] = take(found, mine, other, 5 + n)


def distance(chip):
    return lax.rem(chip - group_index() + 8, 4)


def window_kernel(left, first, inner, last, right, out, wide):
    at = 0
    for ref in (left, first, inner, last, right):
        wide[at : at + ref.shape[0]] = ref[...]
        at += ref.shape[0]
    for chip in range(CHIPS):
        away = distance(chip)
        start = jnp.where(away == 1, STARTS[1], jnp.where(away == 3, STARTS[3], STARTS[0]))
        value = wide[pl.ds(start, WIN)]
        for half in range(2):
            out[2 * chip + half] = value


def clear_kernel(pattern, ready, out, flags, zeros, sem):
    zeros[...] = jnp.zeros_like(zeros)
    copies = [
        pltpu.make_async_copy(zeros, out.at[pl.ds(k * BS, BS)], sem.at[k]) for k in range(4)
    ]
    for copy in copies:
        copy.start()
    row_half = chip_index() // 4
    base = group_index() * 8
    for row in range(-2, 10):
        for col in range(max(-2, row - 2), min(9, row + 2) + 1):
            for half in range(2):
                i = lax.rem(base + row + 32, 32) + 32 * row_half
                j = lax.rem(base + col + 32, 32) + 32 * half
                flags[row + 2, 2 * (col + 2) + half] = pattern[i, j]
    for copy in copies:
        copy.wait()


def purify_kernel(flags_in, mine, other, cleared, out, flags, squares, rounded, result, sem):
    fetch = pltpu.make_async_copy(flags_in, flags, sem.at[4])
    fetch.start()
    core = lax.axis_index("core")
    yh = lax.axis_index("yh")
    zh = lax.axis_index("zh")
    chip = chip_index()
    away = distance(chip)
    row_half = chip // 4

    def dot(a, b):
        return jnp.dot(a, b, preferred_element_type=jnp.float32)

    def block(ref, n, half):
        rows = [ref[2 * (p + zh if p % 2 == 0 else p - zh) + half, n] for p in range(CHIPS)]
        return jnp.concatenate(rows, 0)

    def kept(row, col, half):
        return flags[row + 2, 2 * (col + 2) + half] != 0

    def work(u, start, rows, results):
        halves = (mine, other) if u == 0 else (other, mine)
        same = row_half == u

        def number(row, col):
            return 2 * col + row + 6 - start

        def column(row, col, half):
            return jnp.concatenate([block(h, number(row, col), half) for h in halves], 0)

        def whole(row, col):
            return jnp.concatenate([column(row, col, half) for half in range(2)], 1)

        def left(row, col):
            n = number(row, col)
            parts = [
                jnp.where(same, block(mine, n, half), block(other, n, half)) for half in range(2)
            ]
            return jnp.concatenate(parts, 1)

        near = lambda a, b, d=1: abs(a - b) <= d
        span = range(-2, 10)
        cols = {a: sorted({k for b, j in results if b == a for k in span if near(k, j) and near(k, a, 2)}) for a in rows}
        copies = []
        for r_at, a in enumerate(rows):
            first = cols[a][0]
            for k in cols[a]:
                ls = [l for l in span if near(l, a) and near(l, k)]
                total = dot(
                    jnp.concatenate([left(a, l) for l in ls], 1),
                    jnp.concatenate([whole(l, k) for l in ls], 0),
                )
                if r_at == 0 and k == first:
                    fetch.wait()
                parts = []
                for half in range(2):
                    part = total[:, half * BS : (half + 1) * BS]
                    parts.append(jnp.where(kept(a, k, half), part, jnp.zeros_like(part)))
                squares[r_at, k - first] = jnp.where(yh == 0, parts[0], parts[1])
                rounded[r_at, k - first] = jnp.concatenate(parts, 1).astype(jnp.bfloat16)
            spots = [(j, r, c) for (b, j), (r, c) in results.items() if b == a]
            for j, r, c in spots:
                ks = [k for k in cols[a] if near(k, j)]
                total = dot(
                    jnp.concatenate([rounded[r_at, k - first] for k in ks], 1),
                    jnp.concatenate([column(k, j, yh) for k in ks], 0),
                )
                value = 3.0 * squares[r_at, j - first] - 2.0 * total
                value = jnp.where(kept(a, j, yh), value, jnp.zeros_like(value))
                result[r, :, c * BS : (c + 1) * BS] = value.astype(jnp.bfloat16)
            r = spots[0][1]
            low, high = min(c for *_, c in spots) * BS, (max(c for *_, c in spots) + 1) * BS
            copies.append(
                pltpu.make_async_copy(
                    result.at[r, :, low:high],
                    out.at[pl.ds(r * BS, BS), low:high],
                    sem.at[r_at],
                )
            )
            copies[-1].start()
        for copy in copies:
            copy.wait()

    for u in range(2):

        @pl.when(jnp.logical_and(away == 0, core == u))
        def _(u=u):
            rows = list(range(4 * u, 4 * u + 4))
            spots = [(a, j) for a in rows for j in range(a - 2, a + 3) if 0 <= j < 8]
            work(u, STARTS[0], rows, {(a, j): (a - 4 * u, j) for a, j in spots})

    @pl.when(jnp.logical_and(away == 1, core == 0))
    def _():
        work(0, STARTS[1], [8, 9], {(8, 6): (0, 6), (8, 7): (0, 7), (9, 7): (1, 7)})

    last = jnp.logical_and(away == 3, core == 1)
    near_one = jnp.logical_or(jnp.logical_and(away == 1, core == 0), last)

    @pl.when(jnp.logical_and(away != 0, jnp.logical_not(near_one)))
    def _():
        fetch.wait()

    @pl.when(last)
    def _():
        work(1, STARTS[3], [-1, -2], {(-1, 1): (3, 1), (-1, 0): (3, 0), (-2, 0): (2, 0)})


def to_group(step):
    return [
        (
            ((zl * 2 + g // 2) * 2) + g % 2,
            (((1 - zl) * 2 + (g + step) % 4 // 2) * 2) + (g + step) % 2,
        )
        for zl in range(2)
        for g in range(4)
    ]


def bf16(*shape):
    return jax.ShapeDtypeStruct(shape, jnp.bfloat16)


def call(kernel, out_shape, in_specs, out_specs=VMEM, scratch=(), **options):
    if isinstance(out_shape, list) and not isinstance(out_specs, list):
        out_specs = [out_specs] * len(out_shape)
    return pl.pallas_call(
        kernel,
        out_shape=out_shape,
        in_specs=in_specs,
        out_specs=out_specs,
        scratch_shapes=list(scratch),
        compiler_params=PARAMS,
        **options,
    )


def in_hbm(a):
    return pltpu.with_memory_space_constraint(a, pltpu.HBM)


def swap_cores(a):
    return lax.ppermute(a, "core", [(0, 1), (1, 0)])


def body(built, build_order, p_pattern, q_pattern):
    parts = call(
        pick_kernel,
        bf16(CHIPS, 12, PART, BS),
        [HBM, HBM],
        scratch=[
            pltpu.SMEM((64,), jnp.int32),
            pltpu.VMEM((4, CHIPS, PART, 8 * BS), jnp.bfloat16),
            pltpu.SemaphoreType.DMA((2,)),
        ],
    )(in_hbm(build_order), in_hbm(built.reshape(4, CHIPS, PART, 8 * BS)))
    parts = lax.all_to_all(parts, ("x", "zl"), 0, 0, tiled=True).reshape(PARTS, PART, BS)
    found = call(
        find_kernel,
        jax.ShapeDtypeStruct((24,), jnp.int32),
        [ANY, ANY, ANY],
        SMEM,
        [
            pltpu.SMEM((64,), jnp.int32),
            pltpu.SMEM((24, 64), jnp.int32),
            pltpu.SMEM((64,), jnp.int32),
            pltpu.SemaphoreType.DMA((4,)),
        ],
    )(build_order, p_pattern, parts)
    both = (parts, swap_cores(parts))
    edges = [SMEM, VMEM, VMEM]
    first, last = call(edge_kernel, [bf16(5, PART, BS)] * 2, edges)(found, *both)
    left = lax.ppermute(last, ("zl", "yl", "zh"), to_group(1))
    right = lax.ppermute(first, ("zl", "yl", "zh"), to_group(3))
    inner = call(inner_kernel, bf16(14, PART, BS), edges)(found, *both)
    windows = call(
        window_kernel,
        bf16(2 * CHIPS, WIN, PART, BS),
        [VMEM] * 5,
        scratch=[pltpu.VMEM((WIDE, PART, BS), jnp.bfloat16)],
    )(left, first, inner, last, right)
    windows = lax.all_to_all(windows, ("x", "zl", "yh"), 0, 0, tiled=True)
    cleared, flags = call(
        clear_kernel,
        [pltpu.HBM((4 * BS, 8 * BS), jnp.bfloat16), jax.ShapeDtypeStruct((12, 24), jnp.int32)],
        [SMEM, ANY],
        [HBM, SMEM],
        [pltpu.VMEM((BS, 8 * BS), jnp.bfloat16), pltpu.SemaphoreType.DMA((4,))],
    )(q_pattern, windows)
    return call(
        purify_kernel,
        bf16(4 * BS, 8 * BS),
        [ANY, VMEM, VMEM, HBM],
        HBM,
        [
            pltpu.SMEM((12, 24), jnp.int32),
            pltpu.VMEM((4, 5, BS, BS), jnp.float32),
            pltpu.VMEM((4, 5, BS, 2 * BS), jnp.bfloat16),
            pltpu.VMEM((4, BS, 8 * BS), jnp.bfloat16),
            pltpu.SemaphoreType.DMA((5,)),
        ],
        input_output_aliases={3: 0},
    )(flags, windows, swap_cores(windows), cleared)


def solution(mesh):
    fine = Mesh(mesh.devices.reshape(GRID), AXES)
    placed = (P(ROW, COL), P(), P(), P())
    return jax.shard_map(
        body, mesh=fine, in_specs=placed, out_specs=P(ROW, COL), check_vma=False
    )
```

time: 68.2 us -> 64.9 us (0.952)
  waiting for transfers between devices: 9.5 us -> 2.54 us
  Pallas kernels: 6.98 us -> 10.5 us
  blocking collectives: 41.6 us -> 42.5 us
  starting transfers between devices: 9.74 us -> 9.03 us
    ppermute x2, waiting for transfers between devices: 4.76 us -> 0.41 us  [swap_cores(): return lax.ppermute(a, 'core', [(0, 1), (1, 0)])]
    pallas_call x4 -> x7, Pallas kernels: 6.98 us -> 10.5 us  [the longest x1 3 us: body(): call(clear_kernel, [pltpu.HBM((4 * BS, 8 * BS), jnp.bfloat16), jax.ShapeD...]
    ppermute x2, waiting for transfers between devices: 4.74 us -> 2.13 us  [the longest x1 1.35 us: body(): right = lax.ppermute(first, ('zl', 'yl', 'zh'), to_group(3))]
    all_to_all x1, blocking collectives: 28.5 us -> 29.3 us  [body(): windows = lax.all_to_all(windows, ('x', 'zl', 'yh'), 0, 0, tiled=True)]
    ppermute x2, starting transfers between devices: 5.79 us -> 5 us  [swap_cores(): return lax.ppermute(a, 'core', [(0, 1), (1, 0)])]
  transfers between devices with their start and end apart: 4 -> 4, of which waited for: 4 -> 3; matrix products, arithmetic and copies ran while one was open for 0% -> 0% of each run, Pallas kernels for 0% -> 8%
where the time goes in v3:
time: 64.9 us; the launch traced here: 64.6 us
  blocking collectives  42.5 us (65%)
  Pallas kernels  10.5 us (16%)
  starting transfers between devices  9.03 us (14%)
  waiting for transfers between devices  2.54 us (4%)
    all_to_all x1, blocking collectives, body(): windows = lax.all_to_all(windows, ('x', 'zl', 'yh'), 0, 0, tiled=True)  29.3 us
    all_to_all x1, blocking collectives, body(): lax.all_to_all(parts, ('x', 'zl'), 0, 0, tiled=True)  13.2 us
    ppermute x2, starting transfers between devices, swap_cores(): return lax.ppermute(a, 'core', [(0, 1), (1, 0)])  5 us
    pallas_call x1, Pallas kernels, body(): call(clear_kernel, [pltpu.HBM((4 * BS, 8 * BS), jnp.bfloat16), jax.ShapeD...  3 us
    pallas_call x1, Pallas kernels, body(): call(purify_kernel, bf16(4 * BS, 8 * BS), [ANY, VMEM, VMEM, HBM], HBM, [p...  2.98 us
    ppermute x1, starting transfers between devices, body(): left = lax.ppermute(last, ('zl', 'yl', 'zh'), to_group(1))  2.94 us
    pallas_call x1, Pallas kernels, body(): call(find_kernel, jax.ShapeDtypeStruct((24,), jnp.int32), [ANY, ANY, ANY]...  1.68 us
    pallas_call x1, Pallas kernels, body(): call(pick_kernel, bf16(CHIPS, 12, PART, BS), [HBM, HBM], scratch=[pltpu.S...  1.36 us
  transfers between devices with their start and end apart: 4, of which 3 were waited for; matrix products, arithmetic and copies ran while one was open for 0% of the time, Pallas kernels for 8%

profile of v3, /device:TPU:1, one launch (start us, length us, event | category | flops | bytes accessed | tf_op | source)
XLA Modules:
  0.0 64.6 jit_solution(16648673074519987037)
XLA Ops:
  0.0 0.0 copy-start.2
  0.0 0.0 copy-start.1
  0.0 1.4 %shard_map.46 = bf16[8,12,16,128]{3,2,1,0:T(8,128)(2,1)S(1)} custom-call(s32[64]{0:T(128)} %order_in.1, bf16[4,8,16,1024]{3,2,1,0:T(8,128)(2,1)} %bitcast.6), custom_call_target="tpu_custom_call" | custom-call | tf_op jit(solution)/shard_map/pallas_call | solution.py:293
  1.4 13.2 %all_to_all.10 = bf16[8,12,16,128]{3,2,1,0:T(8,128)(2,1)S(1)} all-to-all(bf16[8,12,16,128]{3,2,1,0:T(8,128)(2,1)S(1)} %shard_map.46), channel_id=1, replica_groups=mesh['x'=4,'zl'=2,'core'=2,'yh'=2,'yl'=2,'zh'=2] {'x','zl'}, dimensions={0} | all-to-all | bytes 786432 | tf_op jit(solution)/shard_map/all_to_all | solution.py:303
  14.5 2.3 %collective-permute-start = (bf16[96,16,128]{2,1,0:T(8,128)(2,1)S(1)}, bf16[96,16,128]{2,1,0:T(8,128)(2,1)S(1)}, u32[]{:S(2)}, u32[]{:S(2)}) collective-permute-start(bf16[96,16,128]{2,1,0:T(8,128)(2,1)S(1)} %bitcast.2), channel_id=1, source_target_pairs={{0,8},{8,0},{1,9},{9,1},{2,10},{10,2},{3,11},{11,3},{4,12},{12,4},... | collective-permute-start | bytes 1179656 | tf_op jit(solution)/shard_map/ppermute | solution.py:289
  16.8 0.0 copy-done.2
  16.8 0.0 copy-done.1
  16.8 1.7 %shard_map.47.found = s32[24]{0:T(128)S(1)} custom-call(s32[64]{0:T(128)S(1)} %copy-done.2, s32[64,64]{1,0:T(8,128)S(1)} %copy-done.1, bf16[96,16,128]{2,1,0:T(8,128)(2,1)S(1)} %bitcast.3), custom_call_target="tpu_custom_call" | custom-call | tf_op jit(solution)/shard_map/pallas_call | solution.py:304
  18.5 0.0 collective-permute-done.other
  18.5 0.6 shard_map.48
  19.1 2.9 %collective-permute-start.1 = (bf16[5,16,128]{2,1,0:T(8,128)(2,1)S(1)}, bf16[5,16,128]{2,1,0:T(8,128)(2,1)S(1)}, u32[]{:S(2)}, u32[]{:S(2)}) collective-permute-start(bf16[5,16,128]{2,1,0:T(8,128)(2,1)S(1)} %get-tuple-element.9.last), channel_id=1, source_target_pairs={{0,17},{1,18},{2,19},{3,16},{16,1},{17,2},{18,3},{19,0},{4,21},{5,... | collective-permute-start | bytes 61448 | tf_op jit(solution)/shard_map/ppermute | solution.py:319
  22.1 1.1 %collective-permute-start.2 = (bf16[5,16,128]{2,1,0:T(8,128)(2,1)S(1)}, bf16[5,16,128]{2,1,0:T(8,128)(2,1)S(1)}, u32[]{:S(2)}, u32[]{:S(2)}) collective-permute-start(bf16[5,16,128]{2,1,0:T(8,128)(2,1)S(1)} %get-tuple-element.10.first), channel_id=1, source_target_pairs={{0,19},{1,16},{2,17},{3,18},{16,3},{17,0},{18,1},{19,2},{4,23},{5,... | collective-permute-start | bytes 61448 | tf_op jit(solution)/shard_map/ppermute | solution.py:320
  23.2 0.6 shard_map.49.inner
  23.8 0.8 %collective-permute-done.1.left = bf16[5,16,128]{2,1,0:T(8,128)(2,1)S(1)} collective-permute-done((bf16[5,16,128]{2,1,0:T(8,128)(2,1)S(1)}, bf16[5,16,128]{2,1,0:T(8,128)(2,1)S(1)}, u32[]{:S(2)}, u32[]{:S(2)}) %collective-permute-start.1) | collective-permute-done | bytes 20512 | tf_op jit(solution)/shard_map/ppermute | solution.py:319
  24.6 1.3 %collective-permute-done.2.right = bf16[5,16,128]{2,1,0:T(8,128)(2,1)S(1)} collective-permute-done((bf16[5,16,128]{2,1,0:T(8,128)(2,1)S(1)}, bf16[5,16,128]{2,1,0:T(8,128)(2,1)S(1)}, u32[]{:S(2)}, u32[]{:S(2)}) %collective-permute-start.2) | collective-permute-done | bytes 20512 | tf_op jit(solution)/shard_map/ppermute | solution.py:320
  25.9 0.3 shard_map.50
  26.2 0.0 copy-start
  26.2 29.3 %all_to_all.11.ready.mine = bf16[16,28,16,128]{3,2,1,0:T(8,128)(2,1)S(1)} all-to-all(bf16[16,28,16,128]{3,2,1,0:T(8,128)(2,1)S(1)} %shard_map.50), channel_id=1, replica_groups=mesh['x'=4,'zl'=2,'core'=2,'yh'=2,'yl'=2,'zh'=2] {'x','zl','yh'}, dimensions={0} | all-to-all | bytes 3670016 | tf_op jit(solution)/shard_map/all_to_all | solution.py:328
  55.5 2.7 %collective-permute-start.3 = (bf16[16,28,16,128]{3,2,1,0:T(8,128)(2,1)S(1)}, bf16[16,28,16,128]{3,2,1,0:T(8,128)(2,1)S(1)}, u32[]{:S(2)}, u32[]{:S(2)}) collective-permute-start(bf16[16,28,16,128]{3,2,1,0:T(8,128)(2,1)S(1)} %all_to_all.11.ready.mine), channel_id=1, source_target_pairs={{0,8},{8,0},{1,9},{9,1},{2,10},{10,2},{3,11},{11,3},{4,12},{12,4},... | collective-permute-start | bytes 5505032 | tf_op jit(solution)/shard_map/ppermute | solution.py:289
  58.2 0.0 copy-done
  58.2 3.0 %shard_map.51 = (bf16[512,1024]{1,0:T(8,128)(2,1)}, s32[12,24]{1,0:T(8,128)S(1)}) custom-call(s32[64,64]{1,0:T(8,128)S(1)} %copy-done, bf16[16,28,16,128]{3,2,1,0:T(8,128)(2,1)S(1)} %all_to_all.11.ready.mine), custom_call_target="tpu_custom_call" | custom-call | tf_op jit(solution)/shard_map/pallas_call | solution.py:329
  61.2 0.4 collective-permute-done.3.other
  61.6 3.0 %shard_map.52 = bf16[512,1024]{1,0:T(8,128)(2,1)} custom-call(s32[12,24]{1,0:T(8,128)S(1)} %get-tuple-element.11.flags_in, bf16[16,28,16,128]{3,2,1,0:T(8,128)(2,1)S(1)} %all_to_all.11.ready.mine, bf16[16,28,16,128]{3,2,1,0:T(8,128)(2,1)S(1)} %collective-permute-done.3.other, bf16[512,1024]{1,0:T(8,128)(2,1)} %get-tuple-element.12.cleared), custom_call_target="tpu_custom_call", output_to_operand_aliasing={{}: (3, {})} | custom-call | tf_op jit(solution)/shard_map/pallas_call | solution.py:336
Async XLA Ops:
  0.0 16.8 %copy-start.2 = (s32[64]{0:T(128)S(1)}, s32[64]{0:T(128)}, u32[]{:S(2)}) copy-start(s32[64]{0:T(128)} %order_in.1) | copy-start | bytes 772
  0.0 16.8 %copy-start.1 = (s32[64,64]{1,0:T(8,128)S(1)}, s32[64,64]{1,0:T(8,128)}, u32[]{:S(2)}) copy-start(s32[64,64]{1,0:T(8,128)} %pattern_in.1) | copy-start | bytes 49156
  14.5 4.0 %collective-permute-start = (bf16[96,16,128]{2,1,0:T(8,128)(2,1)S(1)}, bf16[96,16,128]{2,1,0:T(8,128)(2,1)S(1)}, u32[]{:S(2)}, u32[]{:S(2)}) collective-permute-start(bf16[96,16,128]{2,1,0:T(8,128)(2,1)S(1)} %bitcast.2), channel_id=1, source_target_pairs={{0,8},{8,0},{1,9},{9,1},{2,10},{10,2},{3,11},{11,3},{4,12},{12,4},... | collective-permute-start | bytes 1179656 | tf_op jit(solution)/shard_map/ppermute | solution.py:289
  19.1 5.4 %collective-permute-start.1 = (bf16[5,16,128]{2,1,0:T(8,128)(2,1)S(1)}, bf16[5,16,128]{2,1,0:T(8,128)(2,1)S(1)}, u32[]{:S(2)}, u32[]{:S(2)}) collective-permute-start(bf16[5,16,128]{2,1,0:T(8,128)(2,1)S(1)} %get-tuple-element.9.last), channel_id=1, source_target_pairs={{0,17},{1,18},{2,19},{3,16},{16,1},{17,2},{18,3},{19,0},{4,21},{5,... | collective-permute-start | bytes 61448 | tf_op jit(solution)/shard_map/ppermute | solution.py:319
  22.1 3.8 %collective-permute-start.2 = (bf16[5,16,128]{2,1,0:T(8,128)(2,1)S(1)}, bf16[5,16,128]{2,1,0:T(8,128)(2,1)S(1)}, u32[]{:S(2)}, u32[]{:S(2)}) collective-permute-start(bf16[5,16,128]{2,1,0:T(8,128)(2,1)S(1)} %get-tuple-element.10.first), channel_id=1, source_target_pairs={{0,19},{1,16},{2,17},{3,18},{16,3},{17,0},{18,1},{19,2},{4,23},{5,... | collective-permute-start | bytes 61448 | tf_op jit(solution)/shard_map/ppermute | solution.py:320
  26.2 32.0 %copy-start = (s32[64,64]{1,0:T(8,128)S(1)}, s32[64,64]{1,0:T(8,128)}, u32[]{:S(2)}) copy-start(s32[64,64]{1,0:T(8,128)} %pattern.1) | copy-start | bytes 49156
  55.5 6.1 %collective-permute-start.3 = (bf16[16,28,16,128]{3,2,1,0:T(8,128)(2,1)S(1)}, bf16[16,28,16,128]{3,2,1,0:T(8,128)(2,1)S(1)}, u32[]{:S(2)}, u32[]{:S(2)}) collective-permute-start(bf16[16,28,16,128]{3,2,1,0:T(8,128)(2,1)S(1)} %all_to_all.11.ready.mine), channel_id=1, source_target_pairs={{0,8},{8,0},{1,9},{9,1},{2,10},{10,2},{3,11},{11,3},{4,12},{12,4},... | collective-permute-start | bytes 5505032 | tf_op jit(solution)/shard_map/ppermute | solution.py:289

commit v4 on v3

--- a/solution.py
+++ b/solution.py
@@ -19,7 +19,7 @@
 PARTS = CHIPS * 12
 WIDE = 34
 WIN = 28
-STARTS = (3, 6, 3, 0)
+SHARED = 18
 
 VMEM = pl.BlockSpec(memory_space=pltpu.VMEM)
 SMEM = pl.BlockSpec(memory_space=pltpu.SMEM)
@@ -57,20 +57,22 @@
                 out[chip + 1, 3 * k + d] = built_v[k, chip + 1 - zh, :, at]
 
 
-def find_kernel(order_in, pattern_in, ready, out, order, pattern, inverse, sem):
+def search(order_in, pattern_in, order, pattern, inverse, sem):
     core = lax.axis_index("core")
     yh = lax.axis_index("yh")
     base = group_index() * 8
     copies = [pltpu.make_async_copy(order_in, order, sem.at[0])]
-    for n in range(3):
-        rows = lax.rem(base + 8 * n + 24, 32) + 32 * core
-        copies.append(
-            pltpu.make_async_copy(
-                pattern_in.at[pl.ds(pl.multiple_of(rows, 8), 8)],
-                pattern.at[pl.ds(8 * n, 8)],
-                sem.at[1 + n],
+    for half in range(2):
+        for n in range(3):
+            rows = lax.rem(base + 8 * n + 24, 32) + 32 * half
+            to = 3 * half + n
+            copies.append(
+                pltpu.make_async_copy(
+                    pattern_in.at[pl.ds(pl.multiple_of(rows, 8), 8)],
+                    pattern.at[pl.ds(8 * to, 8)],
+                    sem.at[1 + to],
+                )
             )
-        )
     for copy in copies:
         copy.start()
     copies[0].wait()
@@ -78,19 +80,36 @@
         inverse[order[k]] = k
     for copy in copies[1:]:
         copy.wait()
-    for bl in range(8):
-        for e in range(3):
-            row = lax.rem(base + bl + e + 31, 32) + 32 * core
-            at = inverse[row]
-            device = at // 4
-            slot = (device // 2) * 12 + lax.rem(at, 4) * 3 + (2 - e)
-            slot = jnp.where(lax.rem(device, 2) == core, slot, slot + PARTS)
-            keep = pattern[7 + bl + e, base + bl + 32 * yh] != 0
-            out[3 * bl + e] = jnp.where(keep, slot, 2 * PARTS)
-
-
-def take(found, mine, other, n):
-    at = found[n]
+
+    def find(half, n):
+        bl, e = (n // 3, n % 3) if isinstance(n, int) else (lax.div(n, 3), lax.rem(n, 3))
+        at = inverse[lax.rem(base + bl + e + 31, 32) + 32 * half]
+        device = at // 4
+        slot = (device // 2) * 12 + lax.rem(at, 4) * 3 + (2 - e)
+        slot = jnp.where(lax.rem(device, 2) == core, slot, slot + PARTS)
+        keep = pattern[24 * half + 7 + bl + e, base + bl + 32 * yh] != 0
+        return jnp.where(keep, slot, 2 * PARTS)
+
+    return find
+
+
+SEARCH = [
+    pltpu.SMEM((64,), jnp.int32),
+    pltpu.SMEM((48, 64), jnp.int32),
+    pltpu.SMEM((64,), jnp.int32),
+    pltpu.SemaphoreType.DMA((7,)),
+]
+
+
+def edge_find_kernel(order_in, pattern_in, ready, out, *scratch):
+    find = search(order_in, pattern_in, *scratch)
+    first = 19 * (1 - lax.axis_index("core"))
+    for half in range(2):
+        for n in range(5):
+            out[5 * half + n] = find(half, first + n)
+
+
+def take(at, mine, other):
     here = at < PARTS
     at_mine = jnp.where(here, at, 0)
     at_other = jnp.where(jnp.logical_and(at >= PARTS, at < 2 * PARTS), at - PARTS, 0)
@@ -98,49 +117,71 @@
     return jnp.where(at < 2 * PARTS, value, jnp.zeros_like(value))
 
 
-def edge_kernel(found, mine, other, first, last):
-    for n in range(5):
-        first[n] = take(found, mine, other, n)
-        last[n] = take(found, mine, other, 19 + n)
-
-
-def inner_kernel(found, mine, other, out):
-    for n in range(14):
-        out[n] = take(found, mine, other, 5 + n)
+def edge_kernel(found, mine, other, out):
+    for n in range(10):
+        out[n] = take(found[n], mine, other)
+
+
+def own_kernel(order_in, pattern_in, mine, other, edge, out, *scratch):
+    find = search(order_in, pattern_in, *scratch)
+    for half in range(2):
+        for n in range(24):
+            out[24 * half + n] = take(find(half, n), mine, other)
+
+
+def flags_kernel(pattern_in, ready, flags, pattern, sem):
+    base = group_index() * 8
+    copies = []
+    for n in range(3):
+        rows = lax.rem(base + 8 * n + 24, 32) + 32 * (chip_index() // 4)
+        copies.append(
+            pltpu.make_async_copy(
+                pattern_in.at[pl.ds(pl.multiple_of(rows, 8), 8)],
+                pattern.at[pl.ds(8 * n, 8)],
+                sem.at[n],
+            )
+        )
+        copies[-1].start()
+    for copy in copies:
+        copy.wait()
+    for row in range(-2, 10):
+        for col in range(max(-2, row - 2), min(9, row + 2) + 1):
+            j = lax.rem(base + col + 32, 32)
+            for half in range(2):
+                flags[row + 2, 2 * (col + 2) + half] = pattern[8 + row, j + 32 * half]
 
 
 def distance(chip):
     return lax.rem(chip - group_index() + 8, 4)
 
 
-def window_kernel(left, first, inner, last, right, out, wide):
-    at = 0
-    for ref in (left, first, inner, last, right):
-        wide[at : at + ref.shape[0]] = ref[...]
-        at += ref.shape[0]
+def window_kernel(beside, own, ready, out, wide):
+    for half in range(2):
+        wide[half, 0:5] = beside[5 * half : 5 * half + 5]
+        wide[half, 5:29] = own[24 * half : 24 * half + 24]
+        wide[half, 29:34] = beside[5 * half : 5 * half + 5]
+    core = lax.axis_index("core")
     for chip in range(CHIPS):
         away = distance(chip)
-        start = jnp.where(away == 1, STARTS[1], jnp.where(away == 3, STARTS[3], STARTS[0]))
-        value = wide[pl.ds(start, WIN)]
+        right, left = away == 1, away == 3
+        edge = jnp.logical_or(right, left)
+        pick = lambda r, l, other: jnp.where(right, r, jnp.where(left, l, other))
+        alone = pick(24, 5, 3 + 19 * core)
         for half in range(2):
-            out[2 * chip + half] = value
-
-
-def clear_kernel(pattern, ready, out, flags, zeros, sem):
+            at = 2 * chip + half
+            for h in range(2):
+                out[at, 9 * h : 9 * h + 9] = wide[h, pl.ds(alone, 9)]
+                shared = wide[jnp.where(edge, h, core), pl.ds(pick(29, 0, 12 + 5 * h), 5)]
+                out[at, SHARED + 5 * h : SHARED + 5 * h + 5] = shared
+
+
+def clear_kernel(ready, out, zeros, sem):
     zeros[...] = jnp.zeros_like(zeros)
     copies = [
         pltpu.make_async_copy(zeros, out.at[pl.ds(k * BS, BS)], sem.at[k]) for k in range(4)
     ]
     for copy in copies:
         copy.start()
-    row_half = chip_index() // 4
-    base = group_index() * 8
-    for row in range(-2, 10):
-        for col in range(max(-2, row - 2), min(9, row + 2) + 1):
-            for half in range(2):
-                i = lax.rem(base + row + 32, 32) + 32 * row_half
-                j = lax.rem(base + col + 32, 32) + 32 * half
-                flags[row + 2, 2 * (col + 2) + half] = pattern[i, j]
     for copy in copies:
         copy.wait()
 
@@ -165,23 +206,29 @@
     def kept(row, col, half):
         return flags[row + 2, 2 * (col + 2) + half] != 0
 
-    def work(u, start, rows, results):
-        halves = (mine, other) if u == 0 else (other, mine)
-        same = row_half == u
+    def work(locate, rows, results):
+        def half_block(f, h, half):
+            n = locate(f, h)
+            return block(mine, n, half) if n >= 0 else block(other, n + 10, half)
 
         def number(row, col):
-            return 2 * col + row + 6 - start
+            return 2 * col + row + 6
 
         def column(row, col, half):
-            return jnp.concatenate([block(h, number(row, col), half) for h in halves], 0)
+            return jnp.concatenate([half_block(number(row, col), h, half) for h in range(2)], 0)
 
         def whole(row, col):
             return jnp.concatenate([column(row, col, half) for half in range(2)], 1)
 
         def left(row, col):
-            n = number(row, col)
+            f = number(row, col)
+            low, high = locate(f, 0), locate(f, 1)
+            if low >= 0 and high >= 0:
+                n = low + row_half * (high - low)
+                return jnp.concatenate([block(mine, n, half) for half in range(2)], 1)
             parts = [
-                jnp.where(same, block(mine, n, half), block(other, n, half)) for half in range(2)
+                jnp.where(row_half == 0, half_block(f, 0, half), half_block(f, 1, half))
+                for half in range(2)
             ]
             return jnp.concatenate(parts, 1)
 
@@ -228,17 +275,29 @@
         for copy in copies:
             copy.wait()
 
-    for u in range(2):
+    def low(f, h):
+        return f - 3 + 9 * h if f < 12 else SHARED + f - 12 if h == 0 else f - 22
+
+    def high(f, h):
+        return f - 22 + 9 * h if f > 21 else SHARED + f - 12 if h == 1 else f - 22
+
+    def beyond(f, h):
+        return f - 24 + 9 * h if f < 29 else f - 39 + 5 * h
+
+    def before(f, h):
+        return f - 5 + 9 * h if f > 4 else f - 10 + 5 * h
+
+    for u, locate in enumerate((low, high)):
 
         @pl.when(jnp.logical_and(away == 0, core == u))
-        def _(u=u):
+        def _(u=u, locate=locate):
             rows = list(range(4 * u, 4 * u + 4))
             spots = [(a, j) for a in rows for j in range(a - 2, a + 3) if 0 <= j < 8]
-            work(u, STARTS[0], rows, {(a, j): (a - 4 * u, j) for a, j in spots})
+            work(locate, rows, {(a, j): (a - 4 * u, j) for a, j in spots})
 
     @pl.when(jnp.logical_and(away == 1, core == 0))
     def _():
-        work(0, STARTS[1], [8, 9], {(8, 6): (0, 6), (8, 7): (0, 7), (9, 7): (1, 7)})
+        work(beyond, [8, 9], {(8, 6): (0, 6), (8, 7): (0, 7), (9, 7): (1, 7)})
 
     last = jnp.logical_and(away == 3, core == 1)
     near_one = jnp.logical_or(jnp.logical_and(away == 1, core == 0), last)
@@ -249,16 +308,15 @@
 
     @pl.when(last)
     def _():
-        work(1, STARTS[3], [-1, -2], {(-1, 1): (3, 1), (-1, 0): (3, 0), (-2, 0): (2, 0)})
-
-
-def to_group(step):
+        work(before, [-1, -2], {(-1, 1): (3, 1), (-1, 0): (3, 0), (-2, 0): (2, 0)})
+
+
+def to_groups():
+    index = lambda zl, core, g: (zl * 2 + core) * 4 + g % 4
     return [
-        (
-            ((zl * 2 + g // 2) * 2) + g % 2,
-            (((1 - zl) * 2 + (g + step) % 4 // 2) * 2) + (g + step) % 2,
-        )
+        (index(zl, core, g), index(1 - zl, core, g + (3 if core else 1)))
         for zl in range(2)
+        for core in range(2)
         for g in range(4)
     ]
 
@@ -302,36 +360,34 @@
     )(in_hbm(build_order), in_hbm(built.reshape(4, CHIPS, PART, 8 * BS)))
     parts = lax.all_to_all(parts, ("x", "zl"), 0, 0, tiled=True).reshape(PARTS, PART, BS)
     found = call(
-        find_kernel,
-        jax.ShapeDtypeStruct((24,), jnp.int32),
-        [ANY, ANY, ANY],
-        SMEM,
-        [
-            pltpu.SMEM((64,), jnp.int32),
-            pltpu.SMEM((24, 64), jnp.int32),
-            pltpu.SMEM((64,), jnp.int32),
-            pltpu.SemaphoreType.DMA((4,)),
-        ],
+        edge_find_kernel, jax.ShapeDtypeStruct((10,), jnp.int32), [ANY] * 3, SMEM, SEARCH
     )(build_order, p_pattern, parts)
     both = (parts, swap_cores(parts))
-    edges = [SMEM, VMEM, VMEM]
-    first, last = call(edge_kernel, [bf16(5, PART, BS)] * 2, edges)(found, *both)
-    left = lax.ppermute(last, ("zl", "yl", "zh"), to_group(1))
-    right = lax.ppermute(first, ("zl", "yl", "zh"), to_group(3))
-    inner = call(inner_kernel, bf16(14, PART, BS), edges)(found, *both)
+    edge = call(edge_kernel, bf16(10, PART, BS), [SMEM, VMEM, VMEM])(found, *both)
+    beside = lax.ppermute(edge, ("zl", "core", "yl", "zh"), to_groups())
+    own = call(
+        own_kernel, bf16(48, PART, BS), [ANY, ANY, VMEM, VMEM, ANY], scratch=SEARCH
+    )(build_order, p_pattern, *both, edge)
+    cleared = call(
+        clear_kernel,
+        pltpu.HBM((4 * BS, 8 * BS), jnp.bfloat16),
+        [ANY],
+        HBM,
+        [pltpu.VMEM((BS, 8 * BS), jnp.bfloat16), pltpu.SemaphoreType.DMA((4,))],
+    )(edge)
     windows = call(
         window_kernel,
         bf16(2 * CHIPS, WIN, PART, BS),
-        [VMEM] * 5,
-        scratch=[pltpu.VMEM((WIDE, PART, BS), jnp.bfloat16)],
-    )(left, first, inner, last, right)
+        [VMEM, VMEM, HBM],
+        scratch=[pltpu.VMEM((2, WIDE, PART, BS), jnp.bfloat16)],
+    )(beside, own, in_hbm(cleared))
     windows = lax.all_to_all(windows, ("x", "zl", "yh"), 0, 0, tiled=True)
-    cleared, flags = call(
-        clear_kernel,
-        [pltpu.HBM((4 * BS, 8 * BS), jnp.bfloat16), jax.ShapeDtypeStruct((12, 24), jnp.int32)],
-        [SMEM, ANY],
-        [HBM, SMEM],
-        [pltpu.VMEM((BS, 8 * BS), jnp.bfloat16), pltpu.SemaphoreType.DMA((4,))],
+    flags = call(
+        flags_kernel,
+        jax.ShapeDtypeStruct((12, 24), jnp.int32),
+        [ANY, ANY],
+        SMEM,
+        [pltpu.SMEM((24, 64), jnp.int32), pltpu.SemaphoreType.DMA((3,))],
     )(q_pattern, windows)
     return call(
         purify_kernel,
@@ -346,7 +402,7 @@
             pltpu.SemaphoreType.DMA((5,)),
         ],
         input_output_aliases={3: 0},
-    )(flags, windows, swap_cores(windows), cleared)
+    )(flags, windows, swap_cores(windows[:, SHARED:]), cleared)
 
 
 def solution(mesh):

time: 64.9 us -> 63.3 us (0.975)
  waiting for transfers between devices: 2.54 us -> 0.1 us
  starting transfers between devices: 9.03 us -> 7.88 us
  blocking collectives: 42.5 us -> 43.5 us
  Pallas kernels: 10.5 us -> 11.4 us
    ppermute x2 -> x1, waiting for transfers between devices: 2.13 us -> 0.01 us  [body(): beside = lax.ppermute(edge, ('zl', 'core', 'yl', 'zh'), to_groups())]
    ppermute x2, starting transfers between devices: 5 us -> 3.92 us  [swap_cores(): return lax.ppermute(a, 'core', [(0, 1), (1, 0)])]
    all_to_all x1, blocking collectives: 29.3 us -> 30.3 us  [body(): windows = lax.all_to_all(windows, ('x', 'zl', 'yh'), 0, 0, tiled=True)]
    pallas_call x5 -> x6, Pallas kernels: 6.13 us -> 7.1 us  [the longest x1 1.82 us: body(): call(own_kernel, bf16(48, PART, BS), [ANY, ANY, VMEM, VMEM, ANY], scratch...]
    ppermute x2 -> x1, starting transfers between devices: 4.03 us -> 3.95 us  [body(): beside = lax.ppermute(edge, ('zl', 'core', 'yl', 'zh'), to_groups())]
  transfers between devices with their start and end apart: 4 -> 3, of which waited for: 3 -> 1; matrix products, arithmetic and copies ran while one was open for 0% -> 0% of each run, Pallas kernels for 8% -> 10%
where the time goes in v4:
time: 63.3 us; the launch traced here: 63.1 us
  blocking collectives  43.5 us (69%)
  Pallas kernels  11.4 us (18%)
  starting transfers between devices  7.88 us (12%)
    all_to_all x1, blocking collectives, body(): windows = lax.all_to_all(windows, ('x', 'zl', 'yh'), 0, 0, tiled=True)  30.3 us
    all_to_all x1, blocking collectives, body(): lax.all_to_all(parts, ('x', 'zl'), 0, 0, tiled=True)  13.2 us
    ppermute x1, starting transfers between devices, body(): beside = lax.ppermute(edge, ('zl', 'core', 'yl', 'zh'), to_groups())  3.95 us
    ppermute x2, starting transfers between devices, swap_cores(): return lax.ppermute(a, 'core', [(0, 1), (1, 0)])  3.92 us
    pallas_call x1, Pallas kernels, body(): call(purify_kernel, bf16(4 * BS, 8 * BS), [ANY, VMEM, VMEM, HBM], HBM, [p...  2.97 us
    pallas_call x1, Pallas kernels, body(): call(own_kernel, bf16(48, PART, BS), [ANY, ANY, VMEM, VMEM, ANY], scratch...  1.82 us
    pallas_call x1, Pallas kernels, body(): call(edge_find_kernel, jax.ShapeDtypeStruct((10,), jnp.int32), [ANY] * 3,...  1.76 us
    pallas_call x1, Pallas kernels, body(): call(flags_kernel, jax.ShapeDtypeStruct((12, 24), jnp.int32), [ANY, ANY],...  1.62 us
  transfers between devices with their start and end apart: 3, of which 1 were waited for; matrix products, arithmetic and copies ran while one was open for 0% of the time, Pallas kernels for 10%

profile of v4, /device:TPU:1, one launch (start us, length us, event | category | flops | bytes accessed | tf_op | source)
XLA Modules:
  0.0 63.1 jit_solution(5738258202777867667)
XLA Ops:
  0.0 0.0 copy-start.2
  0.0 0.0 copy-start
  0.0 1.4 %shard_map.46 = bf16[8,12,16,128]{3,2,1,0:T(8,128)(2,1)S(1)} custom-call(s32[64]{0:T(128)} %order_in.3, bf16[4,8,16,1024]{3,2,1,0:T(8,128)(2,1)} %bitcast.6), custom_call_target="tpu_custom_call" | custom-call | tf_op jit(solution)/shard_map/pallas_call | solution.py:351
  1.4 13.2 %all_to_all.10 = bf16[8,12,16,128]{3,2,1,0:T(8,128)(2,1)S(1)} all-to-all(bf16[8,12,16,128]{3,2,1,0:T(8,128)(2,1)S(1)} %shard_map.46), channel_id=1, replica_groups=mesh['x'=4,'zl'=2,'core'=2,'yh'=2,'yl'=2,'zh'=2] {'x','zl'}, dimensions={0} | all-to-all | bytes 786432 | tf_op jit(solution)/shard_map/all_to_all | solution.py:361
  14.5 2.3 %collective-permute-start = (bf16[96,16,128]{2,1,0:T(8,128)(2,1)S(1)}, bf16[96,16,128]{2,1,0:T(8,128)(2,1)S(1)}, u32[]{:S(2)}, u32[]{:S(2)}) collective-permute-start(bf16[96,16,128]{2,1,0:T(8,128)(2,1)S(1)} %bitcast.2), channel_id=1, source_target_pairs={{0,8},{8,0},{1,9},{9,1},{2,10},{10,2},{3,11},{11,3},{4,12},{12,4},... | collective-permute-start | bytes 1179656 | tf_op jit(solution)/shard_map/ppermute | solution.py:347
  16.8 0.0 copy-done.2
  16.8 0.0 copy-done
  16.8 1.8 %shard_map.47.found = s32[10]{0:T(128)S(1)} custom-call(s32[64]{0:T(128)S(1)} %copy-done.2, s32[64,64]{1,0:T(8,128)S(1)} %copy-done, bf16[96,16,128]{2,1,0:T(8,128)(2,1)S(1)} %bitcast.3), custom_call_target="tpu_custom_call" | custom-call | tf_op jit(solution)/shard_map/pallas_call | solution.py:362
  18.6 0.0 collective-permute-done.other
  18.6 0.6 shard_map.48.edge.ready
  19.2 4.0 %collective-permute-start.1 = (bf16[10,16,128]{2,1,0:T(8,128)(2,1)S(1)}, bf16[10,16,128]{2,1,0:T(8,128)(2,1)S(1)}, u32[]{:S(2)}, u32[]{:S(2)}) collective-permute-start(bf16[10,16,128]{2,1,0:T(8,128)(2,1)S(1)} %shard_map.48.edge.ready), channel_id=1, source_target_pairs={{0,17},{1,18},{2,19},{3,16},{8,27},{9,24},{10,25},{11,26},{16,1},{... | collective-permute-start | bytes 122888 | tf_op jit(solution)/shard_map/ppermute | solution.py:367
  23.2 1.0 %shard_map.50.ready.cleared = bf16[512,1024]{1,0:T(8,128)(2,1)} custom-call(bf16[10,16,128]{2,1,0:T(8,128)(2,1)S(1)} %shard_map.48.edge.ready), custom_call_target="tpu_custom_call" | custom-call | tf_op jit(solution)/shard_map/pallas_call | solution.py:371
  24.2 1.8 %shard_map.49.own = bf16[48,16,128]{2,1,0:T(8,128)(2,1)S(1)} custom-call(s32[64]{0:T(128)S(1)} %copy-done.2, s32[64,64]{1,0:T(8,128)S(1)} %copy-done, bf16[96,16,128]{2,1,0:T(8,128)(2,1)S(1)} %bitcast.5, bf16[96,16,128]{2,1,0:T(8,128)(2,1)S(1)} %collective-permute-done.other, bf16[10,16,128]{2,1,0:T(8,128)(2,1)S(1)} %shard_map.48.edge.ready), custom_call_target="tpu_custom_call" | custom-call | tf_op jit(solution)/shard_map/pallas_call | solution.py:368
  26.0 0.0 collective-permute-done.1.beside
  26.0 0.3 shard_map.51
  26.3 0.0 copy-start.1
  26.3 30.3 %all_to_all.11.ready.mine = bf16[16,28,16,128]{3,2,1,0:T(8,128)(2,1)S(1)} all-to-all(bf16[16,28,16,128]{3,2,1,0:T(8,128)(2,1)S(1)} %shard_map.51), channel_id=1, replica_groups=mesh['x'=4,'zl'=2,'core'=2,'yh'=2,'yl'=2,'zh'=2] {'x','zl','yh'}, dimensions={0} | all-to-all | bytes 3670016 | tf_op jit(solution)/shard_map/all_to_all | solution.py:384
  56.6 0.1 slice.4
  56.8 1.6 %collective-permute-start.2 = (bf16[16,10,16,128]{3,2,1,0:T(8,128)(2,1)S(1)}, bf16[16,10,16,128]{3,2,1,0:T(8,128)(2,1)S(1)}, u32[]{:S(2)}, u32[]{:S(2)}) collective-permute-start(bf16[16,10,16,128]{3,2,1,0:T(8,128)(2,1)S(1)} %slice.4), channel_id=1, source_target_pairs={{0,8},{8,0},{1,9},{9,1},{2,10},{10,2},{3,11},{11,3},{4,12},{12,4},... | collective-permute-start | bytes 1966088 | tf_op jit(solution)/shard_map/ppermute | solution.py:347
  58.4 0.0 copy-done.1
  58.4 1.6 %shard_map.52.flags_in = s32[12,24]{1,0:T(8,128)S(1)} custom-call(s32[64,64]{1,0:T(8,128)S(1)} %copy-done.1, bf16[16,28,16,128]{3,2,1,0:T(8,128)(2,1)S(1)} %all_to_all.11.ready.mine), custom_call_target="tpu_custom_call" | custom-call | tf_op jit(solution)/shard_map/pallas_call | solution.py:385
  60.0 0.1 collective-permute-done.2.other
  60.1 3.0 %shard_map.53 = bf16[512,1024]{1,0:T(8,128)(2,1)} custom-call(s32[12,24]{1,0:T(8,128)S(1)} %shard_map.52.flags_in, bf16[16,28,16,128]{3,2,1,0:T(8,128)(2,1)S(1)} %all_to_all.11.ready.mine, bf16[16,10,16,128]{3,2,1,0:T(8,128)(2,1)S(1)} %collective-permute-done.2.other, bf16[512,1024]{1,0:T(8,128)(2,1)} %shard_map.50.ready.cleared), custom_call_target="tpu_custom_call", output_to_operand_aliasing={{}: (3, {})} | custom-call | tf_op jit(solution)/shard_map/pallas_call | solution.py:392
Async XLA Ops:
  0.0 16.8 %copy-start.2 = (s32[64]{0:T(128)S(1)}, s32[64]{0:T(128)}, u32[]{:S(2)}) copy-start(s32[64]{0:T(128)} %order_in.3) | copy-start | bytes 772
  0.0 16.8 %copy-start = (s32[64,64]{1,0:T(8,128)S(1)}, s32[64,64]{1,0:T(8,128)}, u32[]{:S(2)}) copy-start(s32[64,64]{1,0:T(8,128)} %pattern_in.4) | copy-start | bytes 49156
  14.5 4.1 %collective-permute-start = (bf16[96,16,128]{2,1,0:T(8,128)(2,1)S(1)}, bf16[96,16,128]{2,1,0:T(8,128)(2,1)S(1)}, u32[]{:S(2)}, u32[]{:S(2)}) collective-permute-start(bf16[96,16,128]{2,1,0:T(8,128)(2,1)S(1)} %bitcast.2), channel_id=1, source_target_pairs={{0,8},{8,0},{1,9},{9,1},{2,10},{10,2},{3,11},{11,3},{4,12},{12,4},... | collective-permute-start | bytes 1179656 | tf_op jit(solution)/shard_map/ppermute | solution.py:347
  19.2 6.8 %collective-permute-start.1 = (bf16[10,16,128]{2,1,0:T(8,128)(2,1)S(1)}, bf16[10,16,128]{2,1,0:T(8,128)(2,1)S(1)}, u32[]{:S(2)}, u32[]{:S(2)}) collective-permute-start(bf16[10,16,128]{2,1,0:T(8,128)(2,1)S(1)} %shard_map.48.edge.ready), channel_id=1, source_target_pairs={{0,17},{1,18},{2,19},{3,16},{8,27},{9,24},{10,25},{11,26},{16,1},{... | collective-permute-start | bytes 122888 | tf_op jit(solution)/shard_map/ppermute | solution.py:367
  26.3 32.1 %copy-start.1 = (s32[64,64]{1,0:T(8,128)S(1)}, s32[64,64]{1,0:T(8,128)}, u32[]{:S(2)}) copy-start(s32[64,64]{1,0:T(8,128)} %pattern_in.5) | copy-start | bytes 49156
  56.8 3.4 %collective-permute-start.2 = (bf16[16,10,16,128]{3,2,1,0:T(8,128)(2,1)S(1)}, bf16[16,10,16,128]{3,2,1,0:T(8,128)(2,1)S(1)}, u32[]{:S(2)}, u32[]{:S(2)}) collective-permute-start(bf16[16,10,16,128]{3,2,1,0:T(8,128)(2,1)S(1)} %slice.4), channel_id=1, source_target_pairs={{0,8},{8,0},{1,9},{9,1},{2,10},{10,2},{3,11},{11,3},{4,12},{12,4},... | collective-permute-start | bytes 1966088 | tf_op jit(solution)/shard_map/ppermute | solution.py:347

commit v5 on v4

--- a/solution.py
+++ b/solution.py
@@ -37,18 +37,17 @@
 
 
 def pick_kernel(order, built, out, order_s, built_v, sem):
-    copies = [
-        pltpu.make_async_copy(order, order_s, sem.at[0]),
-        pltpu.make_async_copy(built, built_v, sem.at[1]),
-    ]
+    fetch = pltpu.make_async_copy(order, order_s, sem.at[4])
+    fetch.start()
+    copies = [pltpu.make_async_copy(built.at[k], built_v.at[k], sem.at[k]) for k in range(4)]
     for copy in copies:
         copy.start()
-    for copy in copies:
-        copy.wait()
+    fetch.wait()
     first = (chip_index() * 2 + lax.axis_index("core")) * 4
     zh = lax.axis_index("zh")
     for k in range(4):
         row = order_s[first + k]
+        copies[k].wait()
         for d in range(3):
             col = lax.rem(row + d + 31, 8)
             at = pl.ds(pl.multiple_of(col * BS, BS), BS)
@@ -253,13 +252,22 @@
                 squares[r_at, k - first] = jnp.where(yh == 0, parts[0], parts[1])
                 rounded[r_at, k - first] = jnp.concatenate(parts, 1).astype(jnp.bfloat16)
             spots = [(j, r, c) for (b, j), (r, c) in results.items() if b == a]
-            for j, r, c in spots:
-                ks = [k for k in cols[a] if near(k, j)]
+            js = [j for j, _, _ in spots]
+            totals = {}
+            for pair in [js[n : n + 2] for n in range(0, len(js), 2)]:
+                ks = [k for k in cols[a] if any(near(k, j) for j in pair)]
+                rights = [
+                    [column(k, j, yh) if near(k, j) else jnp.zeros((2 * BS, BS), jnp.bfloat16) for j in pair]
+                    for k in ks
+                ]
                 total = dot(
                     jnp.concatenate([rounded[r_at, k - first] for k in ks], 1),
-                    jnp.concatenate([column(k, j, yh) for k in ks], 0),
+                    jnp.concatenate([jnp.concatenate(right, 1) for right in rights], 0),
                 )
-                value = 3.0 * squares[r_at, j - first] - 2.0 * total
+                for n, j in enumerate(pair):
+                    totals[j] = total[:, n * BS : (n + 1) * BS]
+            for j, r, c in spots:
+                value = 3.0 * squares[r_at, j - first] - 2.0 * totals[j]
                 value = jnp.where(kept(a, j, yh), value, jnp.zeros_like(value))
                 result[r, :, c * BS : (c + 1) * BS] = value.astype(jnp.bfloat16)
             r = spots[0][1]
@@ -347,6 +355,23 @@
     return lax.ppermute(a, "core", [(0, 1), (1, 0)])
 
 
+def purify_call(flags, windows, other, cleared):
+    return call(
+        purify_kernel,
+        bf16(4 * BS, 8 * BS),
+        [ANY, VMEM, VMEM, HBM],
+        HBM,
+        [
+            pltpu.SMEM((12, 24), jnp.int32),
+            pltpu.VMEM((4, 5, BS, BS), jnp.float32),
+            pltpu.VMEM((4, 5, BS, 2 * BS), jnp.bfloat16),
+            pltpu.VMEM((4, BS, 8 * BS), jnp.bfloat16),
+            pltpu.SemaphoreType.DMA((5,)),
+        ],
+        input_output_aliases={3: 0},
+    )(flags, windows, other, cleared)
+
+
 def body(built, build_order, p_pattern, q_pattern):
     parts = call(
         pick_kernel,
@@ -355,7 +380,7 @@
         scratch=[
             pltpu.SMEM((64,), jnp.int32),
             pltpu.VMEM((4, CHIPS, PART, 8 * BS), jnp.bfloat16),
-            pltpu.SemaphoreType.DMA((2,)),
+            pltpu.SemaphoreType.DMA((5,)),
         ],
     )(in_hbm(build_order), in_hbm(built.reshape(4, CHIPS, PART, 8 * BS)))
     parts = lax.all_to_all(parts, ("x", "zl"), 0, 0, tiled=True).reshape(PARTS, PART, BS)
@@ -389,20 +414,7 @@
         SMEM,
         [pltpu.SMEM((24, 64), jnp.int32), pltpu.SemaphoreType.DMA((3,))],
     )(q_pattern, windows)
-    return call(
-        purify_kernel,
-        bf16(4 * BS, 8 * BS),
-        [ANY, VMEM, VMEM, HBM],
-        HBM,
-        [
-            pltpu.SMEM((12, 24), jnp.int32),
-            pltpu.VMEM((4, 5, BS, BS), jnp.float32),
-            pltpu.VMEM((4, 5, BS, 2 * BS), jnp.bfloat16),
-            pltpu.VMEM((4, BS, 8 * BS), jnp.bfloat16),
-            pltpu.SemaphoreType.DMA((5,)),
-        ],
-        input_output_aliases={3: 0},
-    )(flags, windows, swap_cores(windows[:, SHARED:]), cleared)
+    return purify_call(flags, windows, swap_cores(windows[:, SHARED:]), cleared)
 
 
 def solution(mesh):

time: 63.3 us -> 63.1 us (level)
  no operation moved by 1% of the time
where the time goes in v5:
time: 63.1 us; the launch traced here: 62.9 us
  blocking collectives  43.5 us (69%)
  Pallas kernels  11.2 us (18%)
  starting transfers between devices  7.88 us (12%)
    all_to_all x1, blocking collectives, body(): windows = lax.all_to_all(windows, ('x', 'zl', 'yh'), 0, 0, tiled=True)  30.3 us
    all_to_all x1, blocking collectives, body(): lax.all_to_all(parts, ('x', 'zl'), 0, 0, tiled=True)  13.2 us
    ppermute x1, starting transfers between devices, body(): beside = lax.ppermute(edge, ('zl', 'core', 'yl', 'zh'), to_groups())  3.95 us
    ppermute x2, starting transfers between devices, swap_cores(): return lax.ppermute(a, 'core', [(0, 1), (1, 0)])  3.92 us
    pallas_call x1, Pallas kernels, purify_call(): call(purify_kernel, bf16(4 * BS, 8 * BS), [ANY, VMEM, VMEM, HBM], HBM, [p...  2.83 us
    pallas_call x1, Pallas kernels, body(): call(own_kernel, bf16(48, PART, BS), [ANY, ANY, VMEM, VMEM, ANY], scratch...  1.82 us
    pallas_call x1, Pallas kernels, body(): call(edge_find_kernel, jax.ShapeDtypeStruct((10,), jnp.int32), [ANY] * 3,...  1.76 us
    pallas_call x1, Pallas kernels, body(): call(flags_kernel, jax.ShapeDtypeStruct((12, 24), jnp.int32), [ANY, ANY],...  1.62 us
  transfers between devices with their start and end apart: 3, of which 1 were waited for; matrix products, arithmetic and copies ran while one was open for 0% of the time, Pallas kernels for 10%

profile of v5, /device:TPU:1, one launch (start us, length us, event | category | flops | bytes accessed | tf_op | source)
XLA Modules:
  0.0 62.9 jit_solution(6016291093575409817)
XLA Ops:
  0.0 0.0 copy-start.2
  0.0 0.0 copy-start
  0.0 1.3 %shard_map.46 = bf16[8,12,16,128]{3,2,1,0:T(8,128)(2,1)S(1)} custom-call(s32[64]{0:T(128)} %order_in.3, bf16[4,8,16,1024]{3,2,1,0:T(8,128)(2,1)} %bitcast.6), custom_call_target="tpu_custom_call" | custom-call | tf_op jit(solution)/shard_map/pallas_call | solution.py:376
  1.3 13.2 %all_to_all.10 = bf16[8,12,16,128]{3,2,1,0:T(8,128)(2,1)S(1)} all-to-all(bf16[8,12,16,128]{3,2,1,0:T(8,128)(2,1)S(1)} %shard_map.46), channel_id=1, replica_groups=mesh['x'=4,'zl'=2,'core'=2,'yh'=2,'yl'=2,'zh'=2] {'x','zl'}, dimensions={0} | all-to-all | bytes 786432 | tf_op jit(solution)/shard_map/all_to_all | solution.py:386
  14.4 2.3 %collective-permute-start = (bf16[96,16,128]{2,1,0:T(8,128)(2,1)S(1)}, bf16[96,16,128]{2,1,0:T(8,128)(2,1)S(1)}, u32[]{:S(2)}, u32[]{:S(2)}) collective-permute-start(bf16[96,16,128]{2,1,0:T(8,128)(2,1)S(1)} %bitcast.2), channel_id=1, source_target_pairs={{0,8},{8,0},{1,9},{9,1},{2,10},{10,2},{3,11},{11,3},{4,12},{12,4},... | collective-permute-start | bytes 1179656 | tf_op jit(solution)/shard_map/ppermute | solution.py:355
  16.7 0.0 copy-done.2
  16.7 0.0 copy-done
  16.7 1.8 %shard_map.47.found = s32[10]{0:T(128)S(1)} custom-call(s32[64]{0:T(128)S(1)} %copy-done.2, s32[64,64]{1,0:T(8,128)S(1)} %copy-done, bf16[96,16,128]{2,1,0:T(8,128)(2,1)S(1)} %bitcast.3), custom_call_target="tpu_custom_call" | custom-call | tf_op jit(solution)/shard_map/pallas_call | solution.py:387
  18.5 0.0 collective-permute-done.other
  18.5 0.6 shard_map.48.edge.ready
  19.1 4.0 %collective-permute-start.1 = (bf16[10,16,128]{2,1,0:T(8,128)(2,1)S(1)}, bf16[10,16,128]{2,1,0:T(8,128)(2,1)S(1)}, u32[]{:S(2)}, u32[]{:S(2)}) collective-permute-start(bf16[10,16,128]{2,1,0:T(8,128)(2,1)S(1)} %shard_map.48.edge.ready), channel_id=1, source_target_pairs={{0,17},{1,18},{2,19},{3,16},{8,27},{9,24},{10,25},{11,26},{16,1},{... | collective-permute-start | bytes 122888 | tf_op jit(solution)/shard_map/ppermute | solution.py:392
  23.1 1.0 %shard_map.50.ready.cleared = bf16[512,1024]{1,0:T(8,128)(2,1)} custom-call(bf16[10,16,128]{2,1,0:T(8,128)(2,1)S(1)} %shard_map.48.edge.ready), custom_call_target="tpu_custom_call" | custom-call | tf_op jit(solution)/shard_map/pallas_call | solution.py:396
  24.1 1.8 %shard_map.49.own = bf16[48,16,128]{2,1,0:T(8,128)(2,1)S(1)} custom-call(s32[64]{0:T(128)S(1)} %copy-done.2, s32[64,64]{1,0:T(8,128)S(1)} %copy-done, bf16[96,16,128]{2,1,0:T(8,128)(2,1)S(1)} %bitcast.5, bf16[96,16,128]{2,1,0:T(8,128)(2,1)S(1)} %collective-permute-done.other, bf16[10,16,128]{2,1,0:T(8,128)(2,1)S(1)} %shard_map.48.edge.ready), custom_call_target="tpu_custom_call" | custom-call | tf_op jit(solution)/shard_map/pallas_call | solution.py:393
  25.9 0.0 collective-permute-done.1.beside
  25.9 0.3 shard_map.51
  26.2 0.0 copy-start.1
  26.2 30.3 %all_to_all.11.ready.mine = bf16[16,28,16,128]{3,2,1,0:T(8,128)(2,1)S(1)} all-to-all(bf16[16,28,16,128]{3,2,1,0:T(8,128)(2,1)S(1)} %shard_map.51), channel_id=1, replica_groups=mesh['x'=4,'zl'=2,'core'=2,'yh'=2,'yl'=2,'zh'=2] {'x','zl','yh'}, dimensions={0} | all-to-all | bytes 3670016 | tf_op jit(solution)/shard_map/all_to_all | solution.py:409
  56.6 0.1 slice.4
  56.7 1.6 %collective-permute-start.2 = (bf16[16,10,16,128]{3,2,1,0:T(8,128)(2,1)S(1)}, bf16[16,10,16,128]{3,2,1,0:T(8,128)(2,1)S(1)}, u32[]{:S(2)}, u32[]{:S(2)}) collective-permute-start(bf16[16,10,16,128]{3,2,1,0:T(8,128)(2,1)S(1)} %slice.4), channel_id=1, source_target_pairs={{0,8},{8,0},{1,9},{9,1},{2,10},{10,2},{3,11},{11,3},{4,12},{12,4},... | collective-permute-start | bytes 1966088 | tf_op jit(solution)/shard_map/ppermute | solution.py:355
  58.3 0.0 copy-done.1
  58.3 1.6 %shard_map.52.flags_in = s32[12,24]{1,0:T(8,128)S(1)} custom-call(s32[64,64]{1,0:T(8,128)S(1)} %copy-done.1, bf16[16,28,16,128]{3,2,1,0:T(8,128)(2,1)S(1)} %all_to_all.11.ready.mine), custom_call_target="tpu_custom_call" | custom-call | tf_op jit(solution)/shard_map/pallas_call | solution.py:410
  59.9 0.1 collective-permute-done.2.other
  60.0 2.8 %shard_map.53 = bf16[512,1024]{1,0:T(8,128)(2,1)} custom-call(s32[12,24]{1,0:T(8,128)S(1)} %shard_map.52.flags_in, bf16[16,28,16,128]{3,2,1,0:T(8,128)(2,1)S(1)} %all_to_all.11.ready.mine, bf16[16,10,16,128]{3,2,1,0:T(8,128)(2,1)S(1)} %collective-permute-done.2.other, bf16[512,1024]{1,0:T(8,128)(2,1)} %shard_map.50.ready.cleared), custom_call_target="tpu_custom_call", output_to_operand_aliasing={{}: (3, {})} | custom-call | tf_op jit(solution)/shard_map/pallas_call | solution.py:359
Async XLA Ops:
  0.0 16.7 %copy-start.2 = (s32[64]{0:T(128)S(1)}, s32[64]{0:T(128)}, u32[]{:S(2)}) copy-start(s32[64]{0:T(128)} %order_in.3) | copy-start | bytes 772
  0.0 16.7 %copy-start = (s32[64,64]{1,0:T(8,128)S(1)}, s32[64,64]{1,0:T(8,128)}, u32[]{:S(2)}) copy-start(s32[64,64]{1,0:T(8,128)} %pattern_in.4) | copy-start | bytes 49156
  14.4 4.1 %collective-permute-start = (bf16[96,16,128]{2,1,0:T(8,128)(2,1)S(1)}, bf16[96,16,128]{2,1,0:T(8,128)(2,1)S(1)}, u32[]{:S(2)}, u32[]{:S(2)}) collective-permute-start(bf16[96,16,128]{2,1,0:T(8,128)(2,1)S(1)} %bitcast.2), channel_id=1, source_target_pairs={{0,8},{8,0},{1,9},{9,1},{2,10},{10,2},{3,11},{11,3},{4,12},{12,4},... | collective-permute-start | bytes 1179656 | tf_op jit(solution)/shard_map/ppermute | solution.py:355
  19.1 6.8 %collective-permute-start.1 = (bf16[10,16,128]{2,1,0:T(8,128)(2,1)S(1)}, bf16[10,16,128]{2,1,0:T(8,128)(2,1)S(1)}, u32[]{:S(2)}, u32[]{:S(2)}) collective-permute-start(bf16[10,16,128]{2,1,0:T(8,128)(2,1)S(1)} %shard_map.48.edge.ready), channel_id=1, source_target_pairs={{0,17},{1,18},{2,19},{3,16},{8,27},{9,24},{10,25},{11,26},{16,1},{... | collective-permute-start | bytes 122888 | tf_op jit(solution)/shard_map/ppermute | solution.py:392
  26.2 32.1 %copy-start.1 = (s32[64,64]{1,0:T(8,128)S(1)}, s32[64,64]{1,0:T(8,128)}, u32[]{:S(2)}) copy-start(s32[64,64]{1,0:T(8,128)} %pattern_in.5) | copy-start | bytes 49156
  56.7 3.4 %collective-permute-start.2 = (bf16[16,10,16,128]{3,2,1,0:T(8,128)(2,1)S(1)}, bf16[16,10,16,128]{3,2,1,0:T(8,128)(2,1)S(1)}, u32[]{:S(2)}, u32[]{:S(2)}) collective-permute-start(bf16[16,10,16,128]{3,2,1,0:T(8,128)(2,1)S(1)} %slice.4), channel_id=1, source_target_pairs={{0,8},{8,0},{1,9},{9,1},{2,10},{10,2},{3,11},{11,3},{4,12},{12,4},... | collective-permute-start | bytes 1966088 | tf_op jit(solution)/shard_map/ppermute | solution.py:355

commit v6 on v5

--- a/solution.py
+++ b/solution.py
@@ -56,20 +56,19 @@
                 out[chip + 1, 3 * k + d] = built_v[k, chip + 1 - zh, :, at]
 
 
-def search(order_in, pattern_in, order, pattern, inverse, sem):
+def search(tiles, order_in, pattern_in, order, pattern, inverse, sem):
     core = lax.axis_index("core")
     yh = lax.axis_index("yh")
     base = group_index() * 8
     copies = [pltpu.make_async_copy(order_in, order, sem.at[0])]
     for half in range(2):
-        for n in range(3):
+        for n in tiles:
             rows = lax.rem(base + 8 * n + 24, 32) + 32 * half
-            to = 3 * half + n
             copies.append(
                 pltpu.make_async_copy(
                     pattern_in.at[pl.ds(pl.multiple_of(rows, 8), 8)],
-                    pattern.at[pl.ds(8 * to, 8)],
-                    sem.at[1 + to],
+                    pattern.at[pl.ds(pl.multiple_of(24 * half + 8 * n, 8), 8)],
+                    sem.at[len(copies)],
                 )
             )
     for copy in copies:
@@ -101,8 +100,9 @@
 
 
 def edge_find_kernel(order_in, pattern_in, ready, out, *scratch):
-    find = search(order_in, pattern_in, *scratch)
-    first = 19 * (1 - lax.axis_index("core"))
+    ahead = 1 - lax.axis_index("core")
+    find = search((ahead, ahead + 1), order_in, pattern_in, *scratch)
+    first = 19 * ahead
     for half in range(2):
         for n in range(5):
             out[5 * half + n] = find(half, first + n)
@@ -122,7 +122,7 @@
 
 
 def own_kernel(order_in, pattern_in, mine, other, edge, out, *scratch):
-    find = search(order_in, pattern_in, *scratch)
+    find = search(range(3), order_in, pattern_in, *scratch)
     for half in range(2):
         for n in range(24):
             out[24 * half + n] = take(find(half, n), mine, other)

time: 63.1 us -> 63 us (level)
  no operation moved by 1% of the time
where the time goes in v6:
time: 63 us; the launch traced here: 62.7 us
  blocking collectives  43.5 us (69%)
  Pallas kernels  11.1 us (18%)
  starting transfers between devices  7.89 us (13%)
    all_to_all x1, blocking collectives, body(): windows = lax.all_to_all(windows, ('x', 'zl', 'yh'), 0, 0, tiled=True)  30.3 us
    all_to_all x1, blocking collectives, body(): lax.all_to_all(parts, ('x', 'zl'), 0, 0, tiled=True)  13.2 us
    ppermute x1, starting transfers between devices, body(): beside = lax.ppermute(edge, ('zl', 'core', 'yl', 'zh'), to_groups())  3.95 us
    ppermute x2, starting transfers between devices, swap_cores(): return lax.ppermute(a, 'core', [(0, 1), (1, 0)])  3.94 us
    pallas_call x1, Pallas kernels, purify_call(): call(purify_kernel, bf16(4 * BS, 8 * BS), [ANY, VMEM, VMEM, HBM], HBM, [p...  2.83 us
    pallas_call x1, Pallas kernels, body(): call(own_kernel, bf16(48, PART, BS), [ANY, ANY, VMEM, VMEM, ANY], scratch...  1.82 us
    pallas_call x1, Pallas kernels, body(): call(edge_find_kernel, jax.ShapeDtypeStruct((10,), jnp.int32), [ANY] * 3,...  1.63 us
    pallas_call x1, Pallas kernels, body(): call(flags_kernel, jax.ShapeDtypeStruct((12, 24), jnp.int32), [ANY, ANY],...  1.62 us
  transfers between devices with their start and end apart: 3, of which 1 were waited for; matrix products, arithmetic and copies ran while one was open for 0% of the time, Pallas kernels for 10%

profile of v6, /device:TPU:1, one launch (start us, length us, event | category | flops | bytes accessed | tf_op | source)
XLA Modules:
  0.0 62.7 jit_solution(957136939462196151)
XLA Ops:
  0.0 0.0 copy-start.2
  0.0 0.0 copy-start
  0.0 1.3 %shard_map.46 = bf16[8,12,16,128]{3,2,1,0:T(8,128)(2,1)S(1)} custom-call(s32[64]{0:T(128)} %order_in.3, bf16[4,8,16,1024]{3,2,1,0:T(8,128)(2,1)} %bitcast.6), custom_call_target="tpu_custom_call" | custom-call | tf_op jit(solution)/shard_map/pallas_call | solution.py:376
  1.3 13.2 %all_to_all.10 = bf16[8,12,16,128]{3,2,1,0:T(8,128)(2,1)S(1)} all-to-all(bf16[8,12,16,128]{3,2,1,0:T(8,128)(2,1)S(1)} %shard_map.46), channel_id=1, replica_groups=mesh['x'=4,'zl'=2,'core'=2,'yh'=2,'yl'=2,'zh'=2] {'x','zl'}, dimensions={0} | all-to-all | bytes 786432 | tf_op jit(solution)/shard_map/all_to_all | solution.py:386
  14.4 2.3 %collective-permute-start = (bf16[96,16,128]{2,1,0:T(8,128)(2,1)S(1)}, bf16[96,16,128]{2,1,0:T(8,128)(2,1)S(1)}, u32[]{:S(2)}, u32[]{:S(2)}) collective-permute-start(bf16[96,16,128]{2,1,0:T(8,128)(2,1)S(1)} %bitcast.2), channel_id=1, source_target_pairs={{0,8},{8,0},{1,9},{9,1},{2,10},{10,2},{3,11},{11,3},{4,12},{12,4},... | collective-permute-start | bytes 1179656 | tf_op jit(solution)/shard_map/ppermute | solution.py:355
  16.7 0.0 copy-done.2
  16.7 0.0 copy-done
  16.7 1.6 %shard_map.47.found = s32[10]{0:T(128)S(1)} custom-call(s32[64]{0:T(128)S(1)} %copy-done.2, s32[64,64]{1,0:T(8,128)S(1)} %copy-done, bf16[96,16,128]{2,1,0:T(8,128)(2,1)S(1)} %bitcast.3), custom_call_target="tpu_custom_call" | custom-call | tf_op jit(solution)/shard_map/pallas_call | solution.py:387
  18.4 0.0 collective-permute-done.other
  18.4 0.6 shard_map.48.edge.ready
  19.0 4.0 %collective-permute-start.1 = (bf16[10,16,128]{2,1,0:T(8,128)(2,1)S(1)}, bf16[10,16,128]{2,1,0:T(8,128)(2,1)S(1)}, u32[]{:S(2)}, u32[]{:S(2)}) collective-permute-start(bf16[10,16,128]{2,1,0:T(8,128)(2,1)S(1)} %shard_map.48.edge.ready), channel_id=1, source_target_pairs={{0,17},{1,18},{2,19},{3,16},{8,27},{9,24},{10,25},{11,26},{16,1},{... | collective-permute-start | bytes 122888 | tf_op jit(solution)/shard_map/ppermute | solution.py:392
  22.9 1.0 %shard_map.50.ready.cleared = bf16[512,1024]{1,0:T(8,128)(2,1)} custom-call(bf16[10,16,128]{2,1,0:T(8,128)(2,1)S(1)} %shard_map.48.edge.ready), custom_call_target="tpu_custom_call" | custom-call | tf_op jit(solution)/shard_map/pallas_call | solution.py:396
  24.0 1.8 %shard_map.49.own = bf16[48,16,128]{2,1,0:T(8,128)(2,1)S(1)} custom-call(s32[64]{0:T(128)S(1)} %copy-done.2, s32[64,64]{1,0:T(8,128)S(1)} %copy-done, bf16[96,16,128]{2,1,0:T(8,128)(2,1)S(1)} %bitcast.5, bf16[96,16,128]{2,1,0:T(8,128)(2,1)S(1)} %collective-permute-done.other, bf16[10,16,128]{2,1,0:T(8,128)(2,1)S(1)} %shard_map.48.edge.ready), custom_call_target="tpu_custom_call" | custom-call | tf_op jit(solution)/shard_map/pallas_call | solution.py:393
  25.8 0.0 collective-permute-done.1.beside
  25.8 0.3 shard_map.51
  26.1 0.0 copy-start.1
  26.1 30.3 %all_to_all.11.ready.mine = bf16[16,28,16,128]{3,2,1,0:T(8,128)(2,1)S(1)} all-to-all(bf16[16,28,16,128]{3,2,1,0:T(8,128)(2,1)S(1)} %shard_map.51), channel_id=1, replica_groups=mesh['x'=4,'zl'=2,'core'=2,'yh'=2,'yl'=2,'zh'=2] {'x','zl','yh'}, dimensions={0} | all-to-all | bytes 3670016 | tf_op jit(solution)/shard_map/all_to_all | solution.py:409
  56.4 0.1 slice.4
  56.5 1.6 %collective-permute-start.2 = (bf16[16,10,16,128]{3,2,1,0:T(8,128)(2,1)S(1)}, bf16[16,10,16,128]{3,2,1,0:T(8,128)(2,1)S(1)}, u32[]{:S(2)}, u32[]{:S(2)}) collective-permute-start(bf16[16,10,16,128]{3,2,1,0:T(8,128)(2,1)S(1)} %slice.4), channel_id=1, source_target_pairs={{0,8},{8,0},{1,9},{9,1},{2,10},{10,2},{3,11},{11,3},{4,12},{12,4},... | collective-permute-start | bytes 1966088 | tf_op jit(solution)/shard_map/ppermute | solution.py:355
  58.2 0.0 copy-done.1
  58.2 1.6 %shard_map.52.flags_in = s32[12,24]{1,0:T(8,128)S(1)} custom-call(s32[64,64]{1,0:T(8,128)S(1)} %copy-done.1, bf16[16,28,16,128]{3,2,1,0:T(8,128)(2,1)S(1)} %all_to_all.11.ready.mine), custom_call_target="tpu_custom_call" | custom-call | tf_op jit(solution)/shard_map/pallas_call | solution.py:410
  59.8 0.1 collective-permute-done.2.other
  59.9 2.8 %shard_map.53 = bf16[512,1024]{1,0:T(8,128)(2,1)} custom-call(s32[12,24]{1,0:T(8,128)S(1)} %shard_map.52.flags_in, bf16[16,28,16,128]{3,2,1,0:T(8,128)(2,1)S(1)} %all_to_all.11.ready.mine, bf16[16,10,16,128]{3,2,1,0:T(8,128)(2,1)S(1)} %collective-permute-done.2.other, bf16[512,1024]{1,0:T(8,128)(2,1)} %shard_map.50.ready.cleared), custom_call_target="tpu_custom_call", output_to_operand_aliasing={{}: (3, {})} | custom-call | tf_op jit(solution)/shard_map/pallas_call | solution.py:359
Async XLA Ops:
  0.0 16.7 %copy-start.2 = (s32[64]{0:T(128)S(1)}, s32[64]{0:T(128)}, u32[]{:S(2)}) copy-start(s32[64]{0:T(128)} %order_in.3) | copy-start | bytes 772
  0.0 16.7 %copy-start = (s32[64,64]{1,0:T(8,128)S(1)}, s32[64,64]{1,0:T(8,128)}, u32[]{:S(2)}) copy-start(s32[64,64]{1,0:T(8,128)} %pattern_in.4) | copy-start | bytes 49156
  14.4 3.9 %collective-permute-start = (bf16[96,16,128]{2,1,0:T(8,128)(2,1)S(1)}, bf16[96,16,128]{2,1,0:T(8,128)(2,1)S(1)}, u32[]{:S(2)}, u32[]{:S(2)}) collective-permute-start(bf16[96,16,128]{2,1,0:T(8,128)(2,1)S(1)} %bitcast.2), channel_id=1, source_target_pairs={{0,8},{8,0},{1,9},{9,1},{2,10},{10,2},{3,11},{11,3},{4,12},{12,4},... | collective-permute-start | bytes 1179656 | tf_op jit(solution)/shard_map/ppermute | solution.py:355
  19.0 6.8 %collective-permute-start.1 = (bf16[10,16,128]{2,1,0:T(8,128)(2,1)S(1)}, bf16[10,16,128]{2,1,0:T(8,128)(2,1)S(1)}, u32[]{:S(2)}, u32[]{:S(2)}) collective-permute-start(bf16[10,16,128]{2,1,0:T(8,128)(2,1)S(1)} %shard_map.48.edge.ready), channel_id=1, source_target_pairs={{0,17},{1,18},{2,19},{3,16},{8,27},{9,24},{10,25},{11,26},{16,1},{... | collective-permute-start | bytes 122888 | tf_op jit(solution)/shard_map/ppermute | solution.py:392
  26.1 32.1 %copy-start.1 = (s32[64,64]{1,0:T(8,128)S(1)}, s32[64,64]{1,0:T(8,128)}, u32[]{:S(2)}) copy-start(s32[64,64]{1,0:T(8,128)} %pattern_in.5) | copy-start | bytes 49156
  56.5 3.4 %collective-permute-start.2 = (bf16[16,10,16,128]{3,2,1,0:T(8,128)(2,1)S(1)}, bf16[16,10,16,128]{3,2,1,0:T(8,128)(2,1)S(1)}, u32[]{:S(2)}, u32[]{:S(2)}) collective-permute-start(bf16[16,10,16,128]{3,2,1,0:T(8,128)(2,1)S(1)} %slice.4), channel_id=1, source_target_pairs={{0,8},{8,0},{1,9},{9,1},{2,10},{10,2},{3,11},{11,3},{4,12},{12,4},... | collective-permute-start | bytes 1966088 | tf_op jit(solution)/shard_map/ppermute | solution.py:355

commit v7 on v6

--- a/solution.py
+++ b/solution.py
@@ -299,7 +299,7 @@
 
         @pl.when(jnp.logical_and(away == 0, core == u))
         def _(u=u, locate=locate):
-            rows = list(range(4 * u, 4 * u + 4))
+            rows = list(range(4, 8) if u else range(3, -1, -1))
             spots = [(a, j) for a in rows for j in range(a - 2, a + 3) if 0 <= j < 8]
             work(locate, rows, {(a, j): (a - 4 * u, j) for a, j in spots})
 

time: 63 us -> 63 us (level)
  no operation moved by 1% of the time
where the time goes in v7:
time: 63 us; the launch traced here: 62.7 us
  blocking collectives  43.5 us (69%)
  Pallas kernels  11.1 us (18%)
  starting transfers between devices  7.89 us (13%)
    all_to_all x1, blocking collectives, body(): windows = lax.all_to_all(windows, ('x', 'zl', 'yh'), 0, 0, tiled=True)  30.3 us
    all_to_all x1, blocking collectives, body(): lax.all_to_all(parts, ('x', 'zl'), 0, 0, tiled=True)  13.2 us
    ppermute x1, starting transfers between devices, body(): beside = lax.ppermute(edge, ('zl', 'core', 'yl', 'zh'), to_groups())  3.95 us
    ppermute x2, starting transfers between devices, swap_cores(): return lax.ppermute(a, 'core', [(0, 1), (1, 0)])  3.94 us
    pallas_call x1, Pallas kernels, purify_call(): call(purify_kernel, bf16(4 * BS, 8 * BS), [ANY, VMEM, VMEM, HBM], HBM, [p...  2.84 us
    pallas_call x1, Pallas kernels, body(): call(own_kernel, bf16(48, PART, BS), [ANY, ANY, VMEM, VMEM, ANY], scratch...  1.82 us
    pallas_call x1, Pallas kernels, body(): call(edge_find_kernel, jax.ShapeDtypeStruct((10,), jnp.int32), [ANY] * 3,...  1.63 us
    pallas_call x1, Pallas kernels, body(): call(flags_kernel, jax.ShapeDtypeStruct((12, 24), jnp.int32), [ANY, ANY],...  1.62 us
  transfers between devices with their start and end apart: 3, of which 1 were waited for; matrix products, arithmetic and copies ran while one was open for 0% of the time, Pallas kernels for 10%

profile of v7, /device:TPU:1, one launch (start us, length us, event | category | flops | bytes accessed | tf_op | source)
XLA Modules:
  0.0 62.7 jit_solution(14400221184489583513)
XLA Ops:
  0.0 0.0 copy-start.2
  0.0 0.0 copy-start
  0.0 1.3 %shard_map.46 = bf16[8,12,16,128]{3,2,1,0:T(8,128)(2,1)S(1)} custom-call(s32[64]{0:T(128)} %order_in.3, bf16[4,8,16,1024]{3,2,1,0:T(8,128)(2,1)} %bitcast.6), custom_call_target="tpu_custom_call" | custom-call | tf_op jit(solution)/shard_map/pallas_call | solution.py:376
  1.3 13.2 %all_to_all.10 = bf16[8,12,16,128]{3,2,1,0:T(8,128)(2,1)S(1)} all-to-all(bf16[8,12,16,128]{3,2,1,0:T(8,128)(2,1)S(1)} %shard_map.46), channel_id=1, replica_groups=mesh['x'=4,'zl'=2,'core'=2,'yh'=2,'yl'=2,'zh'=2] {'x','zl'}, dimensions={0} | all-to-all | bytes 786432 | tf_op jit(solution)/shard_map/all_to_all | solution.py:386
  14.4 2.3 %collective-permute-start = (bf16[96,16,128]{2,1,0:T(8,128)(2,1)S(1)}, bf16[96,16,128]{2,1,0:T(8,128)(2,1)S(1)}, u32[]{:S(2)}, u32[]{:S(2)}) collective-permute-start(bf16[96,16,128]{2,1,0:T(8,128)(2,1)S(1)} %bitcast.2), channel_id=1, source_target_pairs={{0,8},{8,0},{1,9},{9,1},{2,10},{10,2},{3,11},{11,3},{4,12},{12,4},... | collective-permute-start | bytes 1179656 | tf_op jit(solution)/shard_map/ppermute | solution.py:355
  16.7 0.0 copy-done.2
  16.7 0.0 copy-done
  16.7 1.6 %shard_map.47.found = s32[10]{0:T(128)S(1)} custom-call(s32[64]{0:T(128)S(1)} %copy-done.2, s32[64,64]{1,0:T(8,128)S(1)} %copy-done, bf16[96,16,128]{2,1,0:T(8,128)(2,1)S(1)} %bitcast.3), custom_call_target="tpu_custom_call" | custom-call | tf_op jit(solution)/shard_map/pallas_call | solution.py:387
  18.4 0.0 collective-permute-done.other
  18.4 0.6 shard_map.48.edge.ready
  19.0 4.0 %collective-permute-start.1 = (bf16[10,16,128]{2,1,0:T(8,128)(2,1)S(1)}, bf16[10,16,128]{2,1,0:T(8,128)(2,1)S(1)}, u32[]{:S(2)}, u32[]{:S(2)}) collective-permute-start(bf16[10,16,128]{2,1,0:T(8,128)(2,1)S(1)} %shard_map.48.edge.ready), channel_id=1, source_target_pairs={{0,17},{1,18},{2,19},{3,16},{8,27},{9,24},{10,25},{11,26},{16,1},{... | collective-permute-start | bytes 122888 | tf_op jit(solution)/shard_map/ppermute | solution.py:392
  22.9 1.0 %shard_map.50.ready.cleared = bf16[512,1024]{1,0:T(8,128)(2,1)} custom-call(bf16[10,16,128]{2,1,0:T(8,128)(2,1)S(1)} %shard_map.48.edge.ready), custom_call_target="tpu_custom_call" | custom-call | tf_op jit(solution)/shard_map/pallas_call | solution.py:396
  24.0 1.8 %shard_map.49.own = bf16[48,16,128]{2,1,0:T(8,128)(2,1)S(1)} custom-call(s32[64]{0:T(128)S(1)} %copy-done.2, s32[64,64]{1,0:T(8,128)S(1)} %copy-done, bf16[96,16,128]{2,1,0:T(8,128)(2,1)S(1)} %bitcast.5, bf16[96,16,128]{2,1,0:T(8,128)(2,1)S(1)} %collective-permute-done.other, bf16[10,16,128]{2,1,0:T(8,128)(2,1)S(1)} %shard_map.48.edge.ready), custom_call_target="tpu_custom_call" | custom-call | tf_op jit(solution)/shard_map/pallas_call | solution.py:393
  25.8 0.0 collective-permute-done.1.beside
  25.8 0.3 shard_map.51
  26.1 0.0 copy-start.1
  26.1 30.3 %all_to_all.11.ready.mine = bf16[16,28,16,128]{3,2,1,0:T(8,128)(2,1)S(1)} all-to-all(bf16[16,28,16,128]{3,2,1,0:T(8,128)(2,1)S(1)} %shard_map.51), channel_id=1, replica_groups=mesh['x'=4,'zl'=2,'core'=2,'yh'=2,'yl'=2,'zh'=2] {'x','zl','yh'}, dimensions={0} | all-to-all | bytes 3670016 | tf_op jit(solution)/shard_map/all_to_all | solution.py:409
  56.4 0.1 slice.4
  56.5 1.6 %collective-permute-start.2 = (bf16[16,10,16,128]{3,2,1,0:T(8,128)(2,1)S(1)}, bf16[16,10,16,128]{3,2,1,0:T(8,128)(2,1)S(1)}, u32[]{:S(2)}, u32[]{:S(2)}) collective-permute-start(bf16[16,10,16,128]{3,2,1,0:T(8,128)(2,1)S(1)} %slice.4), channel_id=1, source_target_pairs={{0,8},{8,0},{1,9},{9,1},{2,10},{10,2},{3,11},{11,3},{4,12},{12,4},... | collective-permute-start | bytes 1966088 | tf_op jit(solution)/shard_map/ppermute | solution.py:355
  58.2 0.0 copy-done.1
  58.2 1.6 %shard_map.52.flags_in = s32[12,24]{1,0:T(8,128)S(1)} custom-call(s32[64,64]{1,0:T(8,128)S(1)} %copy-done.1, bf16[16,28,16,128]{3,2,1,0:T(8,128)(2,1)S(1)} %all_to_all.11.ready.mine), custom_call_target="tpu_custom_call" | custom-call | tf_op jit(solution)/shard_map/pallas_call | solution.py:410
  59.8 0.1 collective-permute-done.2.other
  59.9 2.8 %shard_map.53 = bf16[512,1024]{1,0:T(8,128)(2,1)} custom-call(s32[12,24]{1,0:T(8,128)S(1)} %shard_map.52.flags_in, bf16[16,28,16,128]{3,2,1,0:T(8,128)(2,1)S(1)} %all_to_all.11.ready.mine, bf16[16,10,16,128]{3,2,1,0:T(8,128)(2,1)S(1)} %collective-permute-done.2.other, bf16[512,1024]{1,0:T(8,128)(2,1)} %shard_map.50.ready.cleared), custom_call_target="tpu_custom_call", output_to_operand_aliasing={{}: (3, {})} | custom-call | tf_op jit(solution)/shard_map/pallas_call | solution.py:359
Async XLA Ops:
  0.0 16.7 %copy-start.2 = (s32[64]{0:T(128)S(1)}, s32[64]{0:T(128)}, u32[]{:S(2)}) copy-start(s32[64]{0:T(128)} %order_in.3) | copy-start | bytes 772
  0.0 16.7 %copy-start = (s32[64,64]{1,0:T(8,128)S(1)}, s32[64,64]{1,0:T(8,128)}, u32[]{:S(2)}) copy-start(s32[64,64]{1,0:T(8,128)} %pattern_in.4) | copy-start | bytes 49156
  14.4 3.9 %collective-permute-start = (bf16[96,16,128]{2,1,0:T(8,128)(2,1)S(1)}, bf16[96,16,128]{2,1,0:T(8,128)(2,1)S(1)}, u32[]{:S(2)}, u32[]{:S(2)}) collective-permute-start(bf16[96,16,128]{2,1,0:T(8,128)(2,1)S(1)} %bitcast.2), channel_id=1, source_target_pairs={{0,8},{8,0},{1,9},{9,1},{2,10},{10,2},{3,11},{11,3},{4,12},{12,4},... | collective-permute-start | bytes 1179656 | tf_op jit(solution)/shard_map/ppermute | solution.py:355
  19.0 6.8 %collective-permute-start.1 = (bf16[10,16,128]{2,1,0:T(8,128)(2,1)S(1)}, bf16[10,16,128]{2,1,0:T(8,128)(2,1)S(1)}, u32[]{:S(2)}, u32[]{:S(2)}) collective-permute-start(bf16[10,16,128]{2,1,0:T(8,128)(2,1)S(1)} %shard_map.48.edge.ready), channel_id=1, source_target_pairs={{0,17},{1,18},{2,19},{3,16},{8,27},{9,24},{10,25},{11,26},{16,1},{... | collective-permute-start | bytes 122888 | tf_op jit(solution)/shard_map/ppermute | solution.py:392
  26.1 32.1 %copy-start.1 = (s32[64,64]{1,0:T(8,128)S(1)}, s32[64,64]{1,0:T(8,128)}, u32[]{:S(2)}) copy-start(s32[64,64]{1,0:T(8,128)} %pattern_in.5) | copy-start | bytes 49156
  56.5 3.4 %collective-permute-start.2 = (bf16[16,10,16,128]{3,2,1,0:T(8,128)(2,1)S(1)}, bf16[16,10,16,128]{3,2,1,0:T(8,128)(2,1)S(1)}, u32[]{:S(2)}, u32[]{:S(2)}) collective-permute-start(bf16[16,10,16,128]{3,2,1,0:T(8,128)(2,1)S(1)} %slice.4), channel_id=1, source_target_pairs={{0,8},{8,0},{1,9},{9,1},{2,10},{10,2},{3,11},{11,3},{4,12},{12,4},... | collective-permute-start | bytes 1966088 | tf_op jit(solution)/shard_map/ppermute | solution.py:355
